TPU v7x, 32 devices: a whole 2x2x4 slice. The times are simulated.
32 devices in a mesh: phase: 2 (over x), lat: 2 (over core), lon: 8 (over z, y).
Axes of the slice: x: 2, y: 2, z: 4, core: 2. Of those that a mesh axis runs over, the one named last changes fastest.
Arguments:
- x_in: bfloat16 [2, 2, 12, 96, 512], P('phase', None, 'lat', 'lon'), may hold values from -430 to 430
- out_grad: bfloat16 [2, 2, 12, 96, 512], P('phase', None, 'lat', 'lon'), may hold values from -6 to 6
- w_qkv: bfloat16 [2, 1536, 512], P('phase'), may hold values from -0.25 to 0.25
- w_proj: bfloat16 [2, 512, 512], P('phase'), may hold values from -0.25 to 0.25
- norm_gain: float32 [2, 512], P('phase'), may hold values from 0.25 to 1.75
- bias_table: float32 [2, 8, 759], P('phase'), may hold values from -80 to 165
- lat_labels: int32 [12], P('lat'), may hold values from 0 to 2, never falling along the last dimension, each value on 1 to 8 neighbouring positions
Outputs:
- grad_input: bfloat16 [2, 2, 12, 96, 512], P('phase', None, 'lat', 'lon')
- grad_qkv: float32 [2, 1536, 512], P('phase', 'lat', 'lon')
Inputs may be any that keep to these rules, and one draw needn't show every extreme that they name: `lat_labels`: labels never fall from one latitude row to the next; each label holds 1 to 8 consecutive rows, and one holds 8.
All inputs are finite; a program needn't handle non-finite values.
Results may differ from a plain program's by a relative error of at most 0.028.
Values may be sent and summed in bfloat16 or wider, within the bound.
A program may use at most 64 MiB of HBM per device.

v0:
```python
import jax
import jax.numpy as jnp
from jax import lax
from jax.sharding import PartitionSpec as P

HEADS = 8
WIN_LEV = 2
WIN_LAT = 6
WIN_LON = 12


EPSILON = 1e-05
MASKED = -1e30


def as_sent(array):

    def short(part):
        return part.astype(jnp.bfloat16) if part.dtype == jnp.float32 else part

    return jax.tree.map(short, array)


def passed_along(array, axis, by):
    devices = lax.axis_size(axis)
    return lax.ppermute(array, axis, [(i, (i + by) % devices) for i in range(devices)])


def from_behind(value, axis, steps):
    count = lax.axis_size(axis)
    first, last = (max(0, -steps), min(count, count - steps))
    return lax.ppermute(value, axis, [(source, source + steps) for source in range(first, last)])


def mixing(formula, left_side, right_side):
    return jnp.einsum(formula, left_side, right_side, preferred_element_type=jnp.float32)


def window_split(grid_field):
    levels, lat_rows, lon_cols, features = grid_field.shape
    grid_field = grid_field.reshape(
        levels // WIN_LEV,
        WIN_LEV,
        lat_rows // WIN_LAT,
        WIN_LAT,
        lon_cols // WIN_LON,
        WIN_LON,
        features,
    )
    grid_field = grid_field.transpose(0, 2, 4, 1, 3, 5, 6)
    return grid_field.reshape(-1, WIN_LEV * WIN_LAT * WIN_LON, features)


def window_merge(blocks, levels, lat_rows, lon_cols):
    features = blocks.shape[-1]
    grid_field = blocks.reshape(
        levels // WIN_LEV,
        lat_rows // WIN_LAT,
        lon_cols // WIN_LON,
        WIN_LEV,
        WIN_LAT,
        WIN_LON,
        features,
    )
    grid_field = grid_field.transpose(0, 3, 1, 4, 2, 5, 6)
    return grid_field.reshape(levels, lat_rows, lon_cols, features)


def make_tags(labels_shifted, levels, lon_cols):
    position = jnp.arange(levels, dtype=jnp.int32)
    region = jnp.where(position < levels - 2, 0, jnp.where(position == levels - 2, 1, 2)).astype(
        jnp.int32
    )
    tag_grid = 3 * labels_shifted[None, :, None] + region[:, None, None]
    tag_grid = jnp.broadcast_to(tag_grid, (levels, labels_shifted.shape[0], lon_cols))
    return window_split(tag_grid[..., None])[..., 0]


def selector(extent):
    offsets = jnp.arange(extent, dtype=jnp.int32)
    target = offsets[:, None] - offsets[None, :] + extent - 1
    return (
        target[:, :, None] == jnp.arange(2 * extent - 1, dtype=jnp.int32)[None, None, :]
    ).astype(jnp.float32)


def window_bias(rel_table):
    head_count = rel_table.shape[0]
    table_grid = rel_table.reshape(head_count, 2 * WIN_LEV - 1, 2 * WIN_LAT - 1, 2 * WIN_LON - 1)
    highest = lax.Precision.HIGHEST
    step_one = jnp.einsum("habc,pqa->hpqbc", table_grid, selector(WIN_LEV), precision=highest)
    step_two = jnp.einsum("hpqbc,rsb->hpqrsc", step_one, selector(WIN_LAT), precision=highest)
    step_three = jnp.einsum("hpqrsc,tuc->hpqrstu", step_two, selector(WIN_LON), precision=highest)
    cell_count = WIN_LEV * WIN_LAT * WIN_LON
    return step_three.transpose(0, 1, 3, 5, 2, 4, 6).reshape(head_count, cell_count, cell_count)


def recompute(blocks, tag_blocks, qkv_weight, gain_vector, attn_bias):
    window_count, cell_count, features = blocks.shape
    head_dim = features // HEADS
    values_wide = blocks.astype(jnp.float32)
    center = jnp.mean(values_wide, axis=-1, keepdims=True)
    spread = jnp.mean(jnp.square(values_wide - center), axis=-1, keepdims=True)
    inv_std = lax.rsqrt(spread + EPSILON)
    normed = (values_wide - center) * inv_std
    scaled_input = (normed * gain_vector).astype(jnp.bfloat16)
    projected = mixing("wnd,ed->wne", scaled_input, qkv_weight).astype(jnp.bfloat16)
    split_heads = projected.reshape(window_count, cell_count, 3, HEADS, head_dim)
    query_heads = split_heads[:, :, 0]
    key_heads = split_heads[:, :, 1]
    value_heads = split_heads[:, :, 2]
    score_scale = head_dim ** (-0.5)
    scores = mixing("wihc,wjhc->whij", query_heads, key_heads) * score_scale + attn_bias[None]
    allowed = tag_blocks[:, None, :, None] == tag_blocks[:, None, None, :]
    scores = jnp.where(allowed, scores, MASKED)
    row_max = jnp.max(scores, axis=-1, keepdims=True)
    weights = jnp.exp(scores - row_max)
    attention = weights / jnp.sum(weights, axis=-1, keepdims=True)
    return (
        scaled_input,
        normed,
        inv_std,
        query_heads,
        key_heads,
        value_heads,
        attention,
        attention.astype(jnp.bfloat16),
    )


def backprop(stored, grad_blocks, qkv_weight, proj_weight, gain_vector):
    scaled_input, normed, inv_std, query_heads, key_heads, value_heads, attention, attention_low = (
        stored
    )
    window_count, cell_count, features = grad_blocks.shape
    head_dim = features // HEADS
    score_scale = head_dim ** (-0.5)
    d_attended = mixing("wne,ed->wnd", grad_blocks, proj_weight).astype(jnp.bfloat16)
    d_heads = d_attended.reshape(window_count, cell_count, HEADS, head_dim)
    d_probs = mixing("wihc,wjhc->whij", d_heads, value_heads)
    d_value = mixing("whij,wihc->wjhc", attention_low, d_heads)
    inner_sum = jnp.sum(attention * d_probs, axis=-1, keepdims=True)
    d_scores = (attention * (d_probs - inner_sum)).astype(jnp.bfloat16)
    d_query = mixing("whij,wjhc->wihc", d_scores, key_heads) * score_scale
    d_key = mixing("whij,wihc->wjhc", d_scores, query_heads) * score_scale
    d_qkv = jnp.stack([d_query, d_key, d_value], axis=2).reshape(
        window_count, cell_count, 3 * features
    )
    d_normed = mixing("wne,ed->wnd", d_qkv.astype(jnp.bfloat16), qkv_weight) * gain_vector
    d_shifted = inv_std * (
        d_normed
        - jnp.mean(d_normed, axis=-1, keepdims=True)
        - normed * jnp.mean(d_normed * normed, axis=-1, keepdims=True)
    )
    return (d_shifted, d_qkv)


def roll_ahead(fields, labels):
    lat_half = WIN_LAT // 2
    lon_half = WIN_LON // 2
    lon_edges = passed_along(
        as_sent(tuple((member[:, :, :lon_half] for member in fields))), "lon", -1
    )
    joined = tuple(
        (
            jnp.concatenate([member[:, :, lon_half:], edge_part], axis=2)
            for member, edge_part in zip(fields, lon_edges)
        )
    )
    outgoing = tuple((member[:, :lat_half] for member in joined))
    if labels is not None:
        outgoing = outgoing + (labels[:lat_half],)
    arrived = jax.tree.map(
        lambda part, own: part.astype(own.dtype),
        passed_along(as_sent(outgoing), "lat", -1),
        outgoing,
    )
    rolled = tuple(
        (
            jnp.roll(
                jnp.concatenate([member[:, lat_half:], incoming], axis=1), -(WIN_LEV // 2), axis=0
            )
            for member, incoming in zip(joined, arrived)
        )
    )
    if labels is None:
        return (rolled, None)
    return (rolled, jnp.concatenate([labels[lat_half:], arrived[-1]]))


def roll_back(grid_field):
    lat_half = WIN_LAT // 2
    lon_half = WIN_LON // 2
    shifted = jnp.roll(grid_field, WIN_LEV // 2, axis=0)
    arrived = passed_along(shifted[:, -lat_half:].astype(jnp.bfloat16), "lat", 1).astype(
        jnp.float32
    )
    shifted = jnp.concatenate([arrived, shifted[:, :-lat_half]], axis=1)
    arrived = passed_along(as_sent(shifted[:, :, -lon_half:]), "lon", 1)
    return jnp.concatenate([arrived, shifted[:, :, :-lon_half]], axis=2)


def pass_down(values_low):
    return from_behind(values_low, "phase", -1)


def weight_grad(grad_low, flat_input):
    partial_sum = lax.psum_scatter(
        lax.dot_general(
            flat_input, grad_low, (((0,), (0,)), ((), ())), preferred_element_type=jnp.float32
        ).astype(jnp.bfloat16),
        "lon",
        scatter_dimension=0,
        tiled=True,
    )
    result_block = (
        lax.psum_scatter(partial_sum, "lat", scatter_dimension=1, tiled=True).astype(jnp.float32).T
    )
    return result_block


def per_device(x_in, out_grad, w_qkv, w_proj, norm_gain, bias_table, lat_labels):
    levels, lat_rows, lon_cols, features = (
        x_in.shape[1],
        x_in.shape[2],
        x_in.shape[3],
        x_in.shape[4],
    )
    qkv_weight = w_qkv[0]
    proj_weight = w_proj[0]
    gain_vector = norm_gain[0]
    attn_bias = window_bias(bias_table[0])
    rolled, labels_shifted = roll_ahead((x_in[0], out_grad[0]), lat_labels)
    tag_blocks = make_tags(labels_shifted, levels, lon_cols)
    stored = recompute(window_split(rolled[0]), tag_blocks, qkv_weight, gain_vector, attn_bias)
    grad_blocks = window_split(rolled[1])
    first_input, first_qkv = backprop(stored, grad_blocks, qkv_weight, proj_weight, gain_vector)
    first_total = out_grad[0].astype(jnp.float32) + roll_back(
        window_merge(first_input, levels, lat_rows, lon_cols)
    )
    passed = pass_down(first_total.astype(jnp.bfloat16))
    passed_rolled, unused = roll_ahead((passed,), None)
    second_input, second_qkv = backprop(
        stored, window_split(passed_rolled[0]), qkv_weight, proj_weight, gain_vector
    )
    grad_field = first_total + (
        passed.astype(jnp.float32)
        + roll_back(window_merge(second_input, levels, lat_rows, lon_cols))
    )
    grad_input = grad_field.astype(jnp.bfloat16)[None]
    grad_low = (first_qkv + second_qkv).astype(jnp.bfloat16).reshape(-1, 3 * features)
    flat_input = stored[0].reshape(-1, features)
    grad_qkv = weight_grad(grad_low, flat_input)[None]
    return (grad_input, grad_qkv)


def solution(mesh):
    in_specs = (
        P("phase", None, "lat", "lon", None),
        P("phase", None, "lat", "lon", None),
        P("phase", None, None),
        P("phase", None, None),
        P("phase", None),
        P("phase", None, None),
        P("lat"),
    )
    out_specs = (P("phase", None, "lat", "lon", None), P("phase", "lat", "lon"))
    return jax.shard_map(
        per_device, mesh=mesh, in_specs=in_specs, out_specs=out_specs, check_vma=False
    )
```

profile of v0, /device:TPU:0, one launch (start us, length us, event | category | flops | bytes accessed | tf_op | source)
XLA Modules:
  0.0 180.1 jit_solution(16661911995113866261)
XLA Ops:
  7.2 1.1 fusion.67
  8.4 6.1 %collective-permute-start = (bf16[2,6,6,512]{3,0,2,1:T(2,128)(2,1)S(1)}, bf16[2,6,6,512]{3,0,2,1:T(2,128)(2,1)S(1)}, u32[]{:S(2)}, u32[]{:S(2)}) collective-permute-start(bf16[2,6,6,512]{3,0,2,1:T(2,128)(2,1)S(1)} %get-tuple-element.19), channel_id=1, source_target_pairs={{0,7},{1,0},{2,1},{3,2},{4,3},{5,4},{6,5},{7,6},{8,15},{9,8},{10,9... | collective-permute-start | bytes 221192 | tf_op jit(solution)/shard_map/ppermute | solution.py:26
  18.6 5.0 %convolution_bitcast_fusion = f32[8,2,6,12,2,6,12]{6,0,3,5,2,4,1:T(8,128)} fusion(f32[8,2,2,6,6,23,1]{5,4,2,1,0,3,6:T(8,128)S(1)} %convolution_bitcast_fusion.1, s32[12,12]{1,0:T(8,128)S(1)} %subtract_add_fusion), kind=kOutput, calls=%fused_computation.2 | convolution fusion | flops 45788400 | bytes 770112 | tf_op jit(solution)/shard_map/hpqrsc,tuc->hpqrstu/dot_general | solution.py:93
  23.7 13.2 %copy.87 = f32[8,2,6,12,2,6,12]{3,2,1,6,5,4,0:T(8,128)} copy(f32[8,2,6,12,2,6,12]{6,0,3,5,2,4,1:T(8,128)} %convolution_bitcast_fusion) | data formatting | bytes 1327104 | tf_op jit(solution)/shard_map/broadcast_in_dim;reshape | solution.py:113
  36.9 7.5 %reshape.750 = f32[8,144,144]{1,2,0:T(8,128)} reshape(f32[8,2,6,12,2,6,12]{3,2,1,6,5,4,0:T(8,128)} %copy.87) | data formatting | bytes 1327104 | tf_op jit(solution)/shard_map/broadcast_in_dim;reshape | solution.py:113
  52.1 1.6 fusion.8
  53.7 1.2 fusion.70
  55.0 2.9 %convolution_bitcast_fusion.3 = f32[1,144,1,8,64]{1,4,3,2,0:T(8,128)} fusion(bf16[144,8,64]{0,2,1:T(8,128)(2,1)S(1)} %bitcast.158, f32[8,144]{1,0:T(8,128)S(1)} %get-tuple-element.26, f32[8,144,144]{1,2,0:T(8,128)} %copy-done.4), kind=kOutput, calls=%fused_computation.27 | convolution fusion | flops 21732624 | bytes 1110528 | tf_op jit(solution)/shard_map/whij,wihc->wjhc/dot_general | solution.py:36
  57.9 1.3 multiply_reduce_fusion.1
  63.8 1.1 slice.143
  66.7 1.8 collective-permute-start.6
  68.5 5.7 %collective-permute-done.6 = bf16[2,6,6,512]{3,0,2,1:T(2,128)(2,1)S(1)} collective-permute-done((bf16[2,6,6,512]{3,0,2,1:T(2,128)(2,1)S(1)}, bf16[2,6,6,512]{3,0,2,1:T(2,128)(2,1)S(1)}, u32[]{:S(2)}, u32[]{:S(2)}) %collective-permute-start.6) | collective-permute-done | bytes 73760 | tf_op jit(solution)/shard_map/ppermute | solution.py:26
  74.4 1.3 collective-permute-start.7
  75.7 5.9 %collective-permute-done.7 = bf16[2,6,12,512]{3,0,2,1:T(2,128)(2,1)S(1)} collective-permute-done((bf16[2,6,12,512]{3,0,2,1:T(2,128)(2,1)S(1)}, bf16[2,6,12,512]{3,0,2,1:T(2,128)(2,1)S(1)}, u32[]{:S(2)}, u32[]{:S(2)}) %collective-permute-start.7) | collective-permute-done | bytes 147488 | tf_op jit(solution)/shard_map/ppermute | solution.py:32
  81.8 4.3 %collective-permute-done.8 = bf16[2,6,6,512]{3,0,2,1:T(2,128)(2,1)S(1)} collective-permute-done((bf16[2,6,6,512]{3,0,2,1:T(2,128)(2,1)S(1)}, bf16[2,6,6,512]{3,0,2,1:T(2,128)(2,1)S(1)}, u32[]{:S(2)}, u32[]{:S(2)}) %collective-permute-start.8) | collective-permute-done | bytes 73760 | tf_op jit(solution)/shard_map/ppermute | solution.py:26
  86.4 1.3 collective-permute-done.9
  88.3 1.3 convolution_convert_fusion.2
  89.8 2.9 %convolution_bitcast_fusion.2 = f32[1,144,1,8,64]{1,4,3,2,0:T(8,128)} fusion(bf16[144,8,64]{0,2,1:T(8,128)(2,1)S(1)} %bitcast.160, f32[8,144]{1,0:T(8,128)S(1)} %get-tuple-element.26, f32[8,144,144]{1,2,0:T(8,128)} %copy-done.4), kind=kOutput, calls=%fused_computation.26 | convolution fusion | flops 21732624 | bytes 1110528 | tf_op jit(solution)/shard_map/whij,wihc->wjhc/dot_general | solution.py:36
  92.6 1.3 multiply_reduce_fusion
  97.5 1.8 %convolution_convert_fusion = bf16[512,1536]{1,0:T(8,128)(2,1)} fusion(bf16[144,512]{1,0:T(8,128)(2,1)S(1)} %copy-done.14, bf16[144,1536]{0,1:T(8,128)(2,1)S(1)} %bitcast.155), kind=kOutput, calls=%fused_computation.1 | convolution fusion | flops 227278848 | bytes 2162688 | tf_op jit(solution)/shard_map/dot_general | solution.py:209
  101.1 1.1 collective-permute-done.10
  102.3 60.5 %reduce-scatter.3.cloned.1.call-done = bf16[64,1536]{1,0:T(8,128)(2,1)} async-done(((bf16[512,1536]{1,0:T(8,128)(2,1)}), bf16[64,1536]{1,0:T(8,128)(2,1)}) %reduce-scatter.3.cloned.1.call-update) | async-done | bytes 196624 | tf_op jit(solution)/shard_map/reduce_scatter | solution.py:208
  164.2 6.0 %collective-permute-done.11 = bf16[2,6,6,512]{3,0,2,1:T(2,128)(2,1)S(1)} collective-permute-done((bf16[2,6,6,512]{3,0,2,1:T(2,128)(2,1)S(1)}, bf16[2,6,6,512]{3,0,2,1:T(2,128)(2,1)S(1)}, u32[]{:S(2)}, u32[]{:S(2)}) %collective-permute-start.11) | collective-permute-done | bytes 73760 | tf_op jit(solution)/shard_map/ppermute | solution.py:26
  171.6 1.6 convert_bitcast_fusion
  (149 shorter events, 27.4 us)
Async XLA Ops:
  7.2 43.1 %copy-start = (bf16[1,1536,512]{2,1,0:T(8,128)(2,1)S(1)}, bf16[1,1536,512]{2,1,0:T(8,128)(2,1)}, u32[]{:S(2)}) copy-start(bf16[1,1536,512]{2,1,0:T(8,128)(2,1)} %param.9) | copy-start | bytes 4718596
  7.2 155.6 %reduce-scatter.3.cloned.1.call-start = ((), (), s32[]{:S(2)}) async-start(), calls=%async_computation.2 | async-start | bytes 1769472 | tf_op jit(solution)/shard_map/reduce_scatter | solution.py:208
  8.4 36.5 %collective-permute-start = (bf16[2,6,6,512]{3,0,2,1:T(2,128)(2,1)S(1)}, bf16[2,6,6,512]{3,0,2,1:T(2,128)(2,1)S(1)}, u32[]{:S(2)}, u32[]{:S(2)}) collective-permute-start(bf16[2,6,6,512]{3,0,2,1:T(2,128)(2,1)S(1)} %get-tuple-element.19), channel_id=1, source_target_pairs={{0,7},{1,0},{2,1},{3,2},{4,3},{5,4},{6,5},{7,6},{8,15},{9,8},{10,9... | collective-permute-start | bytes 221192 | tf_op jit(solution)/shard_map/ppermute | solution.py:26
  15.5 30.2 %collective-permute-start.3 = (bf16[2,6,6,512]{3,0,2,1:T(2,128)(2,1)S(1)}, bf16[2,6,6,512]{3,0,2,1:T(2,128)(2,1)S(1)}, u32[]{:S(2)}, u32[]{:S(2)}) collective-permute-start(bf16[2,6,6,512]{3,0,2,1:T(2,128)(2,1)S(1)} %get-tuple-element.23), channel_id=1, source_target_pairs={{0,7},{1,0},{2,1},{3,2},{4,3},{5,4},{6,5},{7,6},{8,15},{9,8},{10,9... | collective-permute-start | bytes 221192 | tf_op jit(solution)/shard_map/ppermute | solution.py:26
  16.8 27.7 %collective-permute-start.2 = (s32[3]{0:T(128)S(1)}, s32[3]{0:T(128)S(1)}, u32[]{:S(2)}, u32[]{:S(2)}) collective-permute-start(s32[3]{0:T(128)S(1)} %get-tuple-element.25), channel_id=1, source_target_pairs={{0,8},{8,0},{1,9},{9,1},{2,10},{10,2},{3,11},{11,3},{4,12},{12,4},... | collective-permute-start | bytes 44 | tf_op jit(solution)/shard_map/ppermute | solution.py:26
  45.1 1.5 collective-permute-start.1
  45.9 2.0 %collective-permute-start.4 = (bf16[2,3,12,512]{3,0,2,1:T(2,128)(2,1)S(1)}, bf16[2,3,12,512]{3,0,2,1:T(2,128)(2,1)S(1)}, u32[]{:S(2)}, u32[]{:S(2)}) collective-permute-start(bf16[2,3,12,512]{3,0,2,1:T(2,128)(2,1)S(1)} %get-tuple-element.21), channel_id=1, source_target_pairs={{0,8},{8,0},{1,9},{9,1},{2,10},{10,2},{3,11},{11,3},{4,12},{12,4},... | collective-permute-start | bytes 221192 | tf_op jit(solution)/shard_map/ppermute | solution.py:26
  63.8 10.4 %copy-start.15 = (bf16[1,2,6,12,512]{4,1,3,2,0:T(2,128)(2,1)S(1)}, bf16[1,2,6,12,512]{4,1,3,2,0:T(2,128)(2,1)}, u32[]{:S(2)}) copy-start(bf16[1,2,6,12,512]{4,1,3,2,0:T(2,128)(2,1)} %param.8) | copy-start | bytes 442372
  65.0 1.3 collective-permute-start.5
  66.7 7.5 %collective-permute-start.6 = (bf16[2,6,6,512]{3,0,2,1:T(2,128)(2,1)S(1)}, bf16[2,6,6,512]{3,0,2,1:T(2,128)(2,1)S(1)}, u32[]{:S(2)}, u32[]{:S(2)}) collective-permute-start(bf16[2,6,6,512]{3,0,2,1:T(2,128)(2,1)S(1)} %slice.255), channel_id=1, source_target_pairs={{0,1},{1,2},{2,3},{3,4},{4,5},{5,6},{6,7},{7,0},{8,9},{9,10},{10,1... | collective-permute-start | bytes 221192 | tf_op jit(solution)/shard_map/ppermute | solution.py:26
  68.5 6.0 %copy-start.17 = (f32[2,6,6,512]{3,0,2,1:T(2,128)}, f32[2,6,6,512]{3,0,2,1:T(2,128)S(1)}, u32[]{:S(2)}) copy-start(f32[2,6,6,512]{3,0,2,1:T(2,128)S(1)} %slice.184) | copy-start | bytes 442372
  74.2 1.5 copy-start.19
  74.4 7.2 %collective-permute-start.7 = (bf16[2,6,12,512]{3,0,2,1:T(2,128)(2,1)S(1)}, bf16[2,6,12,512]{3,0,2,1:T(2,128)(2,1)S(1)}, u32[]{:S(2)}, u32[]{:S(2)}) collective-permute-start(bf16[2,6,12,512]{3,0,2,1:T(2,128)(2,1)S(1)} %fusion.59), channel_id=1, source_target_pairs={{16,0},{17,1},{18,2},{19,3},{20,4},{21,5},{22,6},{23,7},{24,8},{25... | collective-permute-start | bytes 442376 | tf_op jit(solution)/shard_map/ppermute | solution.py:32
  81.6 6.0 %copy-start.21 = (bf16[2,6,12,512]{3,0,2,1:T(2,128)(2,1)}, bf16[2,6,12,512]{3,0,2,1:T(2,128)(2,1)S(1)}, u32[]{:S(2)}) copy-start(bf16[2,6,12,512]{3,0,2,1:T(2,128)(2,1)S(1)} %collective-permute-done.7) | copy-start | bytes 442372
  81.7 4.4 %collective-permute-start.8 = (bf16[2,6,6,512]{3,0,2,1:T(2,128)(2,1)S(1)}, bf16[2,6,6,512]{3,0,2,1:T(2,128)(2,1)S(1)}, u32[]{:S(2)}, u32[]{:S(2)}) collective-permute-start(bf16[2,6,6,512]{3,0,2,1:T(2,128)(2,1)S(1)} %get-tuple-element.15), channel_id=1, source_target_pairs={{0,7},{1,0},{2,1},{3,2},{4,3},{5,4},{6,5},{7,6},{8,15},{9,8},{10,9... | collective-permute-start | bytes 221192 | tf_op jit(solution)/shard_map/ppermute | solution.py:26
  86.3 1.3 collective-permute-start.9
  95.1 1.5 copy-start.12
  99.4 72.3 %reduce-scatter.5.cloned.1.call-start = ((), (), s32[]{:S(2)}) async-start(), calls=%async_computation.3 | async-start | bytes 294912 | tf_op jit(solution)/shard_map/reduce_scatter | solution.py:217
  100.5 69.7 %copy-start.16 = (bf16[1,2,6,12,512]{4,1,3,2,0:T(2,128)(2,1)S(1)}, bf16[1,2,6,12,512]{4,1,3,2,0:T(2,128)(2,1)}, u32[]{:S(2)}) copy-start(bf16[1,2,6,12,512]{4,1,3,2,0:T(2,128)(2,1)} %param.8) | copy-start | bytes 442372
  100.5 69.7 %copy-start.18 = (f32[2,6,6,512]{3,0,2,1:T(2,128)S(1)}, f32[2,6,6,512]{3,0,2,1:T(2,128)}, u32[]{:S(2)}) copy-start(f32[2,6,6,512]{3,0,2,1:T(2,128)} %copy-done.17) | copy-start | bytes 442372
  100.5 69.7 %copy-start.20 = (f32[2,6,6,512]{3,0,2,1:T(2,128)S(1)}, f32[2,6,6,512]{3,0,2,1:T(2,128)}, u32[]{:S(2)}) copy-start(f32[2,6,6,512]{3,0,2,1:T(2,128)} %copy-done.19) | copy-start | bytes 442372
  100.6 69.7 %copy-start.22 = (bf16[2,6,12,512]{3,0,2,1:T(2,128)(2,1)S(1)}, bf16[2,6,12,512]{3,0,2,1:T(2,128)(2,1)}, u32[]{:S(2)}) copy-start(bf16[2,6,12,512]{3,0,2,1:T(2,128)(2,1)} %copy-done.21) | copy-start | bytes 442372
  100.9 1.3 collective-permute-start.10
  163.1 7.1 %collective-permute-start.11 = (bf16[2,6,6,512]{3,0,2,1:T(2,128)(2,1)S(1)}, bf16[2,6,6,512]{3,0,2,1:T(2,128)(2,1)S(1)}, u32[]{:S(2)}, u32[]{:S(2)}) collective-permute-start(bf16[2,6,6,512]{3,0,2,1:T(2,128)(2,1)S(1)} %slice.254), channel_id=1, source_target_pairs={{0,1},{1,2},{2,3},{3,4},{4,5},{5,6},{6,7},{7,0},{8,9},{9,10},{10,1... | collective-permute-start | bytes 221192 | tf_op jit(solution)/shard_map/ppermute | solution.py:26
  (14 other events, 14.3 us)
Sparse Core Ops, SparseCore 0:
  99.5 63.2 reduce-scatter.2
  165.1 6.4 reduce-scatter.4
where the time goes:
time: 181 us; the launch traced here: 180 us
  waiting for transfers between devices  86.8 us (48%)
  local copies, waits for them, and re-layouts  34.8 us (19%)
  matrix products  22.2 us (12%)
  between operations  14.7 us (8%)
  starting transfers between devices  12.2 us (7%)
  other arithmetic  9.34 us (5%)
    reduce_scatter x1, waiting for transfers between devices, weight_grad(): lax.psum_scatter(lax.dot_general(flat_input, grad_low, (((0,), (0,)), (()...  60.5 us
    another operation x2, local copies, waits for them, and re-layouts, recompute(): attn_bias[None]  20.8 us
    ppermute x11, waiting for transfers between devices, passed_along(): lax.ppermute(array, axis, [(i, (i + by) % devices) for i in range(devices)])  20 us
    dot_general x14, matrix products, mixing(): jnp.einsum(formula, left_side, right_side, preferred_element_type=jnp.flo...  14.5 us
    ppermute x11, starting transfers between devices, passed_along(): lax.ppermute(array, axis, [(i, (i + by) % devices) for i in range(devices)])  10.8 us
    unnamed x48, local copies, waits for them, and re-layouts  6.19 us
    ppermute x1, waiting for transfers between devices, from_behind(): lax.ppermute(value, axis, [(source, source + steps) for source in range(f...  5.88 us
    dot_general x1, matrix products, window_bias(): jnp.einsum('hpqrsc,tuc->hpqrstu', step_two, selector(WIN_LON), precision=...  5.04 us
  transfers between devices with their start and end apart: 14, of which 10 were waited for; matrix products, arithmetic and copies ran while one was open for 19% of the time, Pallas kernels for 0%

commit v1 on v0

v1 whole, which is shorter than its diff:
```python
import functools

import jax
import jax.numpy as jnp
import ml_dtypes
import numpy as np
from jax import lax
from jax.experimental import pallas as pl
from jax.experimental.pallas import tpu as pltpu
from jax.sharding import PartitionSpec as P

HEADS = 8
EPSILON = 1e-05
MASKED = -1e30
MESH = pl.DeviceIdType.MESH
BF = jnp.bfloat16
F32 = jnp.float32

LEV, LAT, LON = 2, 6, 12
CELLS = LAT * LON
ROWS = 80
WROWS = LEV * ROWS
QROWS = 48
XROWS = LEV * LAT * 16


def permutations():
    to_quadrant = np.zeros((4 * QROWS, XROWS), np.float32)
    to_window = np.zeros((WROWS, 4 * QROWS), np.float32)
    for p in range(LEV):
        for i in range(LAT):
            for j in range(LON):
                ih, ii = divmod(i, LAT // 2)
                jh, jj = divmod(j, LON // 2)
                quad = QROWS * (2 * ih + jh) + 18 * p + 6 * ii + jj
                to_quadrant[quad, 16 * (LAT * p + i) + j] = 1
                row = ROWS * (1 - p) + LON * (ii + 3 * (1 - ih)) + jj + 6 * (1 - jh)
                to_window[row, quad] = 1
    column = np.zeros((128, 128), np.float32)
    label_row = np.zeros((128, 128), np.float32)
    for n in range(CELLS):
        i, j = divmod(n, LON)
        column[126 - (23 * i + j), n] = 1
        label_row[(i + 3) % 6, n] = 1
    return [
        m.astype(ml_dtypes.bfloat16)
        for m in (to_quadrant, to_window, to_window.T, to_quadrant.T, column, label_row)
    ]


def dot(a, b, dims=((1,), (0,))):
    return lax.dot_general(a, b, (dims, ((), ())), preferred_element_type=F32)


NT = ((1,), (1,))
TN = ((0,), (0,))


def kernel(
    n_lat, n_lon, chunk,
    x_ref, og_ref, wqkv_ref, wproj_ref, gain_ref, table_ref, labels_ref,
    to_quad_ref, to_win_ref, from_win_ref, from_quad_ref, column_ref, label_row_ref,
    gin_ref, gq_ref,
    pad_x, pad_og, send_q, recv_q, send_lab, recv_lab, rolled, expanded, bias,
    proj, att, dqkv, cot, skip, back_send, back_recv,
    scaled, scaled_in, low, low_in, part, part_in, summed, summed_in,
    halo_s, halo_r, lab_s, lab_r, skip_s, skip_r, back_s, back_r,
    sc_s, sc_r, low_s, low_r, pair_s, pair_r, grp_s, grp_r,
):
    ph, la, lo = lax.axis_index("phase"), lax.axis_index("lat"), lax.axis_index("lon")
    features = x_ref.shape[-1]
    cols = gq_ref.shape[0]
    rows = gq_ref.shape[1]
    half = n_lon // 2
    chunks = cols // chunk
    par = lax.rem(lo, 2)
    grp = lo // 2

    def device(dlat, dlon):
        return (ph, lax.rem(la + dlat + n_lat, n_lat), lax.rem(lo + dlon + n_lon, n_lon))

    offsets = set()
    for dlat, dlon in ((0, 1), (1, 0), (1, 1)):
        offsets |= {(dlat % n_lat, dlon % n_lon), (-dlat % n_lat, -dlon % n_lon)}
    offsets |= {(d, 0) for d in range(1, n_lat)}
    offsets |= {(0, 2 * d) for d in range(1, half)}
    offsets = sorted(offsets)
    barrier = pltpu.get_barrier_semaphore()
    for dlat, dlon in offsets:
        pl.semaphore_signal(barrier, inc=1, device_id=device(dlat, dlon), device_id_type=MESH)
    pl.semaphore_signal(barrier, inc=1, device_id=(1 - ph, la, lo), device_id_type=MESH)

    pad_x[...] = jnp.zeros_like(pad_x)
    pad_og[...] = jnp.zeros_like(pad_og)
    for k in range(LEV * LAT):
        pad_x[16 * k:16 * k + LON, :] = x_ref[k]
        pad_og[16 * k:16 * k + LON, :] = og_ref[k]
    quad_x = dot(to_quad_ref[...], pad_x[...]).astype(BF)
    quad_og = dot(to_quad_ref[...], pad_og[...]).astype(BF)
    for q in range(4):
        send_q[q, 0] = quad_x[QROWS * q:QROWS * (q + 1)]
        send_q[q, 1] = quad_og[QROWS * q:QROWS * (q + 1)]
    lane = lax.broadcasted_iota(jnp.int32, (8, 128), 1)
    own_lab = jnp.zeros((8, 128), F32)
    for i in range(LAT):
        own_lab = jnp.where(lane == i, labels_ref[i].astype(F32), own_lab)
    send_lab[...] = own_lab

    pl.semaphore_wait(barrier, len(offsets) + 1)

    halo = []
    for q, (dlat, dlon) in enumerate(((-1, -1), (-1, 0), (0, -1))):
        halo.append(pltpu.make_async_remote_copy(
            send_q.at[q], recv_q.at[q], halo_s.at[q], halo_r.at[q],
            device_id=device(dlat, dlon), device_id_type=MESH))
        halo[-1].start()
    lab_copy = pltpu.make_async_remote_copy(
        send_lab, recv_lab, lab_s.at[0], lab_r.at[0],
        device_id=device(-1, 0), device_id_type=MESH)
    lab_copy.start()
    recv_q[3] = send_q[3]

    table = table_ref[:, 128:512]
    for m in range(CELLS):
        i, j = divmod(m, LON)
        shift = (384 - (125 + 23 * i + j)) % 384
        rolled[8 * m:8 * m + 8, :] = pltpu.roll(table, shift, 1)[:, :128]
    wide = rolled[...]
    high = wide.astype(BF)
    rest = wide - high.astype(F32)
    mid = rest.astype(BF)
    least = (rest - mid.astype(F32)).astype(BF)
    column = column_ref[...]
    expanded[...] = (dot(high, column) + dot(mid, column)) + dot(least, column)

    lab_copy.wait()
    lab = jnp.where(lane < 3, recv_lab[...], own_lab)
    lab_row = dot(jnp.concatenate([lab, lab], axis=0).astype(BF), label_row_ref[...])[0:1]
    lane1 = lax.broadcasted_iota(jnp.int32, (1, 128), 1)
    lab_row = jnp.where(lane1 < CELLS, lab_row, -1.0)
    row_id = lax.broadcasted_iota(jnp.int32, (ROWS, 128), 0)
    lane_id = lax.broadcasted_iota(jnp.int32, (ROWS, 128), 1)
    want = jnp.zeros((ROWS, 128), jnp.int32)
    for i in range(LAT):
        want = jnp.where(row_id >= LON * i, (i + 3) % 6, want)
    lab_col = jnp.sum(jnp.where(lane_id == want, lab[0:1], 0.0), axis=1, keepdims=True)
    row1 = lax.broadcasted_iota(jnp.int32, (ROWS, 1), 0)
    lab_col = jnp.where(row1 < CELLS, lab_col, -1.0)
    allowed = lab_col == lab_row
    for h in range(HEADS):
        one = expanded[pl.ds(h, CELLS, stride=8), :]
        one = jnp.concatenate([one, jnp.zeros((ROWS - CELLS, 128), F32)], axis=0)
        bias[h // 2, ROWS * (h % 2):ROWS * (h % 2 + 1), :] = jnp.where(allowed, one, MASKED)

    for copy in halo:
        copy.wait()
    to_win = to_win_ref[...]
    x = dot(to_win, jnp.concatenate([recv_q[q, 0] for q in range(4)], axis=0))
    og = dot(to_win, jnp.concatenate([recv_q[q, 1] for q in range(4)], axis=0))
    gain = gain_ref[...]
    center = jnp.mean(x, axis=-1, keepdims=True)
    spread = jnp.mean(jnp.square(x - center), axis=-1, keepdims=True)
    inv_std = lax.rsqrt(spread + EPSILON)
    normed = (x - center) * inv_std
    scaled[...] = (normed * gain).astype(BF)
    sc_copies = []
    for d in range(1, n_lat):
        sc_copies.append(pltpu.make_async_remote_copy(
            scaled, scaled_in.at[d - 1], sc_s.at[d - 1], sc_r.at[d - 1],
            device_id=device(d, 0), device_id_type=MESH))
        sc_copies[-1].start()
    proj[...] = dot(scaled[...], wqkv_ref[...], NT).astype(BF)
    first_half = lax.broadcasted_iota(jnp.int32, (ROWS, 128), 1) < 64
    zero = jnp.zeros((ROWS, 128), BF)

    def both(pair):
        return jnp.concatenate(
            [jnp.where(first_half, pair, zero), jnp.where(first_half, zero, pair)], axis=0)

    def query_pair(p, hp):
        pair = proj[ROWS * p:ROWS * (p + 1), 128 * hp:128 * (hp + 1)]
        return both(pair * jnp.asarray(0.125, BF))

    def later_pair(which, p, hp):
        start = features * which + 128 * hp
        return proj[ROWS * p:ROWS * (p + 1), start:start + 128]

    for p in range(LEV):
        for hp in range(HEADS // 2):
            scores = dot(query_pair(p, hp), later_pair(1, p, hp), NT) + bias[hp][:, :ROWS]
            weights = jnp.exp(scores - jnp.max(scores, axis=-1, keepdims=True))
            att[4 * p + hp] = weights / jnp.sum(weights, axis=-1, keepdims=True)

    def backprop(cotangent, accumulate):
        d_attended = dot(cotangent, wproj_ref[...]).astype(BF)
        lows = []
        for p in range(LEV):
            parts = [[], [], []]
            for hp in range(HEADS // 2):
                d_pair = both(d_attended[ROWS * p:ROWS * (p + 1), 128 * hp:128 * (hp + 1)])
                attention = att[4 * p + hp]
                d_probs = dot(d_pair, later_pair(2, p, hp), NT)
                d_value = dot(attention.astype(BF), d_pair, TN)
                inner = jnp.sum(attention * d_probs, axis=-1, keepdims=True)
                d_scores = (attention * (d_probs - inner)).astype(BF)
                d_both = dot(d_scores, later_pair(1, p, hp))
                d_query = jnp.where(first_half, d_both[:ROWS], d_both[ROWS:]) * 0.125
                d_key = dot(d_scores, query_pair(p, hp), TN)
                for which, value in enumerate((d_query, d_key, d_value)):
                    start = features * which + 128 * hp
                    parts[which].append(value.astype(BF))
                    at = (slice(ROWS * p, ROWS * (p + 1)), slice(start, start + 128))
                    dqkv[at] = dqkv[at] + value if accumulate else value
            lows.append(jnp.concatenate(parts[0] + parts[1] + parts[2], axis=1))
        d_low = jnp.concatenate(lows, axis=0)
        d_normed = dot(d_low, wqkv_ref[...]) * gain
        return inv_std * (
            d_normed
            - jnp.mean(d_normed, axis=-1, keepdims=True)
            - normed * jnp.mean(d_normed * normed, axis=-1, keepdims=True))

    total = og + backprop(og.astype(BF), False)
    cot[...] = total.astype(BF)
    skip_copy = pltpu.make_async_remote_copy(
        cot, skip, skip_s.at[0], skip_r.at[0],
        device_id=(1 - ph, la, lo), device_id_type=MESH)

    @pl.when(ph == 1)
    def _():
        skip_copy.start()
        skip_copy.wait_send()

    @pl.when(ph == 0)
    def _():
        skip_copy.wait_recv()
        received = skip[...]
        second = backprop(received, True)
        cot[...] = (total + (received.astype(F32) + second)).astype(BF)

    for l in range(n_lat):
        low[l] = dqkv[:, cols * l:cols * (l + 1)].astype(BF)
    low_copies = []
    for d in range(1, n_lat):
        to = device(d, 0)
        low_copies.append(pltpu.make_async_remote_copy(
            low.at[to[1]], low_in.at[d - 1], low_s.at[d - 1], low_r.at[d - 1],
            device_id=to, device_id_type=MESH))
        low_copies[-1].start()

    from_win = dot(from_win_ref[...], cot[...]).astype(BF)
    for q in range(4):
        back_send[q] = from_win[QROWS * q:QROWS * (q + 1)]
    back = []
    for q, (dlat, dlon) in enumerate(((1, 1), (1, 0), (0, 1))):
        back.append(pltpu.make_async_remote_copy(
            back_send.at[q], back_recv.at[q], back_s.at[q], back_r.at[q],
            device_id=device(dlat, dlon), device_id_type=MESH))
    back_recv[3] = back_send[3]

    for copy in sc_copies + low_copies:
        copy.wait()
    pair_to = (ph, la, lo + 1 - 2 * par)
    pairs = []
    for c in range(chunks):
        at = slice(chunk * c, chunk * (c + 1))
        value = dot(scaled[...], low[la][:, at], TN)
        for d in range(1, n_lat):
            value = value + dot(scaled_in[d - 1], low_in[d - 1][:, at], TN)
        value = value.astype(BF)
        for j in range(n_lon):
            part[c, j % 2, j // 2] = value[rows * j:rows * (j + 1)]
        pairs.append(pltpu.make_async_remote_copy(
            part.at[c, 1 - par], part_in.at[c], pair_s.at[c], pair_r.at[c],
            device_id=pair_to, device_id_type=MESH))
        pairs[-1].start()
    for copy in back:
        copy.start()
    groups = []
    for c in range(chunks):
        pairs[c].wait_recv()
        summed[c] = (part[c, par].astype(F32) + part_in[c].astype(F32)).astype(BF)
        for d in range(1, half):
            to = lax.rem(grp + d, half)
            groups.append(pltpu.make_async_remote_copy(
                summed.at[c, to], summed_in.at[c, d - 1],
                grp_s.at[c, d - 1], grp_r.at[c, d - 1],
                device_id=(ph, la, 2 * to + par), device_id_type=MESH))
            groups[-1].start()

    for copy in back:
        copy.wait()
    result = dot(
        from_quad_ref[...], jnp.concatenate([back_recv[q] for q in range(4)], axis=0)).astype(BF)
    for k in range(LEV * LAT):
        gin_ref[k] = result[16 * k:16 * k + LON]

    for copy in groups:
        copy.wait()
    for c in range(chunks):
        value = summed[c, grp].astype(F32)
        for d in range(1, half):
            value = value + summed_in[c, d - 1].astype(F32)
        gq_ref[chunk * c:chunk * (c + 1), :] = value.T
    for copy in pairs:
        copy.wait_send()


def per_device(n_lat, n_lon, x_in, out_grad, w_qkv, w_proj, norm_gain, bias_table, lat_labels):
    features = x_in.shape[-1]
    outs = w_qkv.shape[1]
    cols, rows = outs // n_lat, features // n_lon
    chunk = 256 if cols % 256 == 0 else cols
    chunks, half = cols // chunk, n_lon // 2
    vmem = pl.BlockSpec(memory_space=pltpu.VMEM)
    dma = lambda *shape: pltpu.SemaphoreType.DMA(shape)
    peers = max(n_lat - 1, 1)
    grid = (LEV * LAT, LON, features)
    constants = [jnp.asarray(m) for m in permutations()]
    grad_input, grad_qkv = pl.pallas_call(
        functools.partial(kernel, n_lat, n_lon, chunk),
        out_shape=(
            jax.ShapeDtypeStruct(grid, BF),
            jax.ShapeDtypeStruct((cols, rows), F32),
        ),
        in_specs=[vmem] * 6 + [pl.BlockSpec(memory_space=pltpu.SMEM)] + [vmem] * 6,
        out_specs=(vmem, vmem),
        scratch_shapes=[
            pltpu.VMEM((XROWS, features), BF),
            pltpu.VMEM((XROWS, features), BF),
            pltpu.VMEM((4, 2, QROWS, features), BF),
            pltpu.VMEM((4, 2, QROWS, features), BF),
            pltpu.VMEM((8, 128), F32),
            pltpu.VMEM((8, 128), F32),
            pltpu.VMEM((8 * CELLS, 128), F32),
            pltpu.VMEM((8 * CELLS, 128), F32),
            pltpu.VMEM((HEADS // 2, 2 * ROWS, 128), F32),
            pltpu.VMEM((WROWS, outs), BF),
            pltpu.VMEM((HEADS, 2 * ROWS, ROWS), F32),
            pltpu.VMEM((WROWS, outs), F32),
            pltpu.VMEM((WROWS, features), BF),
            pltpu.VMEM((WROWS, features), BF),
            pltpu.VMEM((4, QROWS, features), BF),
            pltpu.VMEM((4, QROWS, features), BF),
            pltpu.VMEM((WROWS, features), BF),
            pltpu.VMEM((peers, WROWS, features), BF),
            pltpu.VMEM((n_lat, WROWS, cols), BF),
            pltpu.VMEM((peers, WROWS, cols), BF),
            pltpu.VMEM((chunks, 2, half, rows, chunk), BF),
            pltpu.VMEM((chunks, half, rows, chunk), BF),
            pltpu.VMEM((chunks, half, rows, chunk), BF),
            pltpu.VMEM((chunks, half - 1, rows, chunk), BF),
            dma(3), dma(3), dma(1), dma(1), dma(1), dma(1), dma(3), dma(3),
            dma(peers), dma(peers), dma(peers), dma(peers),
            dma(chunks), dma(chunks), dma(chunks, half - 1), dma(chunks, half - 1),
        ],
        compiler_params=pltpu.CompilerParams(
            collective_id=0, has_side_effects=True, vmem_limit_bytes=48 * 1024 * 1024),
    )(
        x_in.reshape(grid), out_grad.reshape(grid), w_qkv[0], w_proj[0], norm_gain,
        bias_table[0], lat_labels, *constants)
    return grad_input.reshape(x_in.shape), grad_qkv[None]


def solution(mesh):
    in_specs = (
        P("phase", None, "lat", "lon", None),
        P("phase", None, "lat", "lon", None),
        P("phase", None, None),
        P("phase", None, None),
        P("phase", None),
        P("phase", None, None),
        P("lat"),
    )
    out_specs = (P("phase", None, "lat", "lon", None), P("phase", "lat", "lon"))
    return jax.shard_map(
        functools.partial(per_device, mesh.shape["lat"], mesh.shape["lon"]),
        mesh=mesh, in_specs=in_specs, out_specs=out_specs, check_vma=False)
```

time: 181 us -> 58.5 us (0.32)
  waiting for transfers between devices: 86.8 us -> 0 us
  Pallas kernels: 0 us -> 44.1 us
  matrix products: 22.2 us -> 0 us
  local copies, waits for them, and re-layouts: 34.8 us -> 13.1 us
  between operations: 14.7 us -> 0.67 us
  starting transfers between devices: 12.2 us -> 0 us
  other arithmetic: 9.34 us -> 0 us
    reduce_scatter x2 -> x0, waiting for transfers between devices: 60.9 us -> none  [the longest x1 60.5 us: weight_grad(): lax.psum_scatter(lax.dot_general(flat_input, grad_low, (((0,), (0,)), (()...]
    pallas_call x0 -> x1, Pallas kernels: none -> 44.1 us  [per_device(): pl.pallas_call(functools.partial(kernel, n_lat, n_lon, chunk), out_shape=...]
    ppermute x12 -> x0, waiting for transfers between devices: 25.8 us -> none  [the longest x11 20 us: passed_along(): lax.ppermute(array, axis, [(i, (i + by) % devices) for i in range(devices)])]
    dot_general x18 -> x0, matrix products: 22.2 us -> none  [the longest x14 14.5 us: mixing(): jnp.einsum(formula, left_side, right_side, preferred_element_type=jnp.flo...]
    another operation x8 -> x0, local copies, waits for them, and re-layouts: 22 us -> none  [the longest x2 20.8 us: recompute(): attn_bias[None]]
    ppermute x12 -> x0, starting transfers between devices: 12.1 us -> none  [the longest x11 10.8 us: passed_along(): lax.ppermute(array, axis, [(i, (i + by) % devices) for i in range(devices)])]
    unnamed x48 -> x26, local copies, waits for them, and re-layouts: 6.19 us -> 13.1 us
    slice x14 -> x0, local copies, waits for them, and re-layouts: 5.52 us -> none  [the longest x6 2.33 us: roll_back(): shifted = jnp.roll(grid_field, WIN_LEV // 2, axis=0)]
  transfers between devices with their start and end apart: 14 -> 0, of which waited for: 10 -> 0; matrix products, arithmetic and copies ran while one was open for 19% -> 0% of each run, Pallas kernels for 0% -> 0%
where the time goes in v1:
time: 58.5 us; the launch traced here: 57.9 us
  Pallas kernels  44.1 us (75%)
  local copies, waits for them, and re-layouts  13.1 us (22%)
  between operations  0.67 us (1%)
    pallas_call x1, Pallas kernels, per_device(): pl.pallas_call(functools.partial(kernel, n_lat, n_lon, chunk), out_shape=...  44.1 us
    unnamed x26, local copies, waits for them, and re-layouts  13.1 us

profile of v1, /device:TPU:0, one launch (start us, length us, event | category | flops | bytes accessed | tf_op | source)
XLA Modules:
  0.0 57.9 jit_solution(11606672361013738360)
XLA Ops:
  0.6 0.9 %copy.15 = bf16[1,2,6,12,512]{4,3,2,1,0:T(8,128)(2,1)S(1)} copy(bf16[1,2,6,12,512]{4,1,3,2,0:T(2,128)(2,1)} %param.13) | data formatting | bytes 294912 | tf_op args[0]
  1.6 0.9 %copy.16 = bf16[1,2,6,12,512]{4,3,2,1,0:T(8,128)(2,1)S(1)} copy(bf16[1,2,6,12,512]{4,1,3,2,0:T(2,128)(2,1)} %param.14) | data formatting | bytes 294912 | tf_op args[1]
  2.5 0.0 copy-start
  2.5 1.4 %copy-done = bf16[1,1536,512]{2,1,0:T(8,128)(2,1)S(1)} copy-done((bf16[1,1536,512]{2,1,0:T(8,128)(2,1)S(1)}, bf16[1,1536,512]{2,1,0:T(8,128)(2,1)}, u32[]{:S(2)}) %copy-start) | copy-done | bytes 1572888
  3.9 0.0 copy-start.1
  3.9 1.0 %copy-done.1 = bf16[1,512,512]{2,1,0:T(8,128)(2,1)S(1)} copy-done((bf16[1,512,512]{2,1,0:T(8,128)(2,1)S(1)}, bf16[1,512,512]{2,1,0:T(8,128)(2,1)}, u32[]{:S(2)}) %copy-start.1) | copy-done | bytes 524312
  5.0 0.0 copy-start.2
  5.0 0.9 %copy-done.2 = bf16[192,192]{1,0:T(8,128)(2,1)S(1)} copy-done((bf16[192,192]{1,0:T(8,128)(2,1)S(1)}, bf16[192,192]{1,0:T(8,128)(2,1)}, u32[]{:S(2)}) %copy-start.2) | copy-done | bytes 73752
  5.9 0.9 %copy-done.3 = bf16[192,160]{1,0:T(8,128)(2,1)S(1)} copy-done((bf16[192,160]{1,0:T(8,128)(2,1)S(1)}, bf16[192,160]{1,0:T(8,128)(2,1)}, u32[]{:S(2)}) %copy-start.3) | copy-done | bytes 61464
  6.8 0.0 copy-start.4
  6.8 0.9 %copy-done.4 = bf16[192,192]{1,0:T(8,128)(2,1)S(1)} copy-done((bf16[192,192]{1,0:T(8,128)(2,1)S(1)}, bf16[192,192]{1,0:T(8,128)(2,1)}, u32[]{:S(2)}) %copy-start.4) | copy-done | bytes 73752
  7.6 0.0 copy-start.5
  7.6 0.9 %copy-done.5 = bf16[160,192]{1,0:T(8,128)(2,1)S(1)} copy-done((bf16[160,192]{1,0:T(8,128)(2,1)S(1)}, bf16[160,192]{1,0:T(8,128)(2,1)}, u32[]{:S(2)}) %copy-start.5) | copy-done | bytes 61464
  8.5 0.0 copy-start.6
  8.5 0.8 %copy-done.6 = bf16[128,128]{1,0:T(8,128)(2,1)S(1)} copy-done((bf16[128,128]{1,0:T(8,128)(2,1)S(1)}, bf16[128,128]{1,0:T(8,128)(2,1)}, u32[]{:S(2)}) %copy-start.6) | copy-done | bytes 32792
  9.3 0.0 copy-start.7
  9.3 0.8 %copy-done.7 = bf16[128,128]{1,0:T(8,128)(2,1)S(1)} copy-done((bf16[128,128]{1,0:T(8,128)(2,1)S(1)}, bf16[128,128]{1,0:T(8,128)(2,1)}, u32[]{:S(2)}) %copy-start.7) | copy-done | bytes 32792
  10.0 0.0 copy-start.8
  10.1 0.7 %copy-done.8 = f32[1,8,759]{2,1,0:T(8,128)S(1)} copy-done((f32[1,8,759]{2,1,0:T(8,128)S(1)}, f32[1,8,759]{2,1,0:T(8,128)}, u32[]{:S(2)}) %copy-start.8) | copy-done | bytes 24312
  10.8 0.7 %copy-done.9 = f32[1,512]{1,0:T(1,128)S(1)} copy-done((f32[1,512]{1,0:T(1,128)S(1)}, f32[1,512]{1,0:T(1,128)}, u32[]{:S(2)}) %copy-start.9) | copy-done | bytes 2072
  11.5 0.7 %copy-done.10 = s32[6]{0:T(128)S(1)} copy-done((s32[6]{0:T(128)S(1)}, s32[6]{0:T(128)}, u32[]{:S(2)}) %copy-start.10) | copy-done | bytes 48
  12.1 44.1 %shard_map.140 = (bf16[12,12,512]{2,1,0:T(8,128)(2,1)S(1)}, f32[768,64]{1,0:T(8,128)S(1)}) custom-call(bf16[12,12,512]{2,1,0:T(8,128)(2,1)S(1)} %bitcast.8, bf16[12,12,512]{2,1,0:T(8,128)(2,1)S(1)} %bitcast.9, bf16[1536,512]{1,0:T(8,128)(2,1)S(1)} %bitcast.7, bf16[512,512]{1,0:T(8,128)(2,1)S(1)} %bitcast.10, f32[1,512]{1,0:T(1,128)S(1)} %copy-done.9, ...), custom_call_target="tpu_custom_call" | custom-call | tf_op jit(solution)/shard_map/pallas_call | solution.py:319
  56.3 0.8 %copy.17 = bf16[1,2,6,12,512]{4,1,3,2,0:T(2,128)(2,1)} copy(bf16[1,2,6,12,512]{4,3,2,1,0:T(8,128)(2,1)S(1)} %bitcast.12) | data formatting | bytes 294912
  57.1 0.8 %copy.18 = f32[1,768,64]{1,2,0:T(8,128)} copy(f32[1,768,64]{2,1,0:T(8,128)S(1)} %bitcast.11) | data formatting | bytes 393216
  (3 shorter events, 0.0 us)
Async XLA Ops:
  2.5 1.4 %copy-start = (bf16[1,1536,512]{2,1,0:T(8,128)(2,1)S(1)}, bf16[1,1536,512]{2,1,0:T(8,128)(2,1)}, u32[]{:S(2)}) copy-start(bf16[1,1536,512]{2,1,0:T(8,128)(2,1)} %param.15) | copy-start | bytes 4718596
  3.9 1.0 %copy-start.1 = (bf16[1,512,512]{2,1,0:T(8,128)(2,1)S(1)}, bf16[1,512,512]{2,1,0:T(8,128)(2,1)}, u32[]{:S(2)}) copy-start(bf16[1,512,512]{2,1,0:T(8,128)(2,1)} %param.16) | copy-start | bytes 1572868
  5.0 0.9 %copy-start.2 = (bf16[192,192]{1,0:T(8,128)(2,1)S(1)}, bf16[192,192]{1,0:T(8,128)(2,1)}, u32[]{:S(2)}) copy-start(bf16[192,192]{1,0:T(8,128)(2,1)} %constant.15.clone.from_quad_ref) | copy-start | bytes 221188
  5.9 0.9 %copy-start.3 = (bf16[192,160]{1,0:T(8,128)(2,1)S(1)}, bf16[192,160]{1,0:T(8,128)(2,1)}, u32[]{:S(2)}) copy-start(bf16[192,160]{1,0:T(8,128)(2,1)} %constant.14.clone.from_win_ref) | copy-start | bytes 184324
  6.8 0.9 %copy-start.4 = (bf16[192,192]{1,0:T(8,128)(2,1)S(1)}, bf16[192,192]{1,0:T(8,128)(2,1)}, u32[]{:S(2)}) copy-start(bf16[192,192]{1,0:T(8,128)(2,1)} %constant.12.clone.to_quad_ref) | copy-start | bytes 221188
  7.6 0.9 %copy-start.5 = (bf16[160,192]{1,0:T(8,128)(2,1)S(1)}, bf16[160,192]{1,0:T(8,128)(2,1)}, u32[]{:S(2)}) copy-start(bf16[160,192]{1,0:T(8,128)(2,1)} %constant.13.clone.to_win_ref) | copy-start | bytes 184324
  8.5 0.8 %copy-start.6 = (bf16[128,128]{1,0:T(8,128)(2,1)S(1)}, bf16[128,128]{1,0:T(8,128)(2,1)}, u32[]{:S(2)}) copy-start(bf16[128,128]{1,0:T(8,128)(2,1)} %constant.17.clone.label_row_ref) | copy-start | bytes 98308
  9.3 0.8 %copy-start.7 = (bf16[128,128]{1,0:T(8,128)(2,1)S(1)}, bf16[128,128]{1,0:T(8,128)(2,1)}, u32[]{:S(2)}) copy-start(bf16[128,128]{1,0:T(8,128)(2,1)} %constant.16.clone.column_ref) | copy-start | bytes 98308
  10.0 0.7 %copy-start.8 = (f32[1,8,759]{2,1,0:T(8,128)S(1)}, f32[1,8,759]{2,1,0:T(8,128)}, u32[]{:S(2)}) copy-start(f32[1,8,759]{2,1,0:T(8,128)} %param.18) | copy-start | bytes 72868
  10.8 0.7 %copy-start.9 = (f32[1,512]{1,0:T(1,128)S(1)}, f32[1,512]{1,0:T(1,128)}, u32[]{:S(2)}) copy-start(f32[1,512]{1,0:T(1,128)} %gain_ref.1) | copy-start | bytes 6148
  11.5 0.7 %copy-start.10 = (s32[6]{0:T(128)S(1)}, s32[6]{0:T(128)}, u32[]{:S(2)}) copy-start(s32[6]{0:T(128)} %labels_ref.1) | copy-start | bytes 76

commit v2 on v1

v2 whole, which is shorter than its diff:
```python
import functools

import jax
import jax.numpy as jnp
import numpy as np
from jax import lax
from jax.experimental import pallas as pl
from jax.experimental.pallas import tpu as pltpu
from jax.sharding import PartitionSpec as P

HEADS = 8
EPSILON = 1e-05
MASKED = -1e30
MESH = pl.DeviceIdType.MESH
BF = jnp.bfloat16
F32 = jnp.float32

LEV, LAT, LON = 2, 6, 12
CELLS = LAT * LON
ROWS = 80
WROWS = LEV * ROWS


def selections():
    packed = np.zeros((WROWS + 256, 256), np.float32)
    for n in range(CELLS):
        i, j = divmod(n, LON)
        for p in range(LEV):
            packed[ROWS * (1 - p) + n, LEV * n + p] = 1
        packed[WROWS + 126 - (23 * i + j), n] = 1
        packed[WROWS + 128 + (i + 3) % 6, n] = 1
    return packed


def dot(a, b, dims=((1,), (0,))):
    return lax.dot_general(a, b, (dims, ((), ())), preferred_element_type=F32)


NT = ((1,), (1,))
TN = ((0,), (0,))


def kernel(
    n_lat, n_lon, chunk,
    x_hbm, og_hbm, wqkv_hbm, wproj_hbm, gain_hbm, table_hbm, labels_hbm, select_hbm,
    gin_ref, gq_ref,
    win_x, win_og, wqkv_ref, wproj_ref, gain_ref, table_ref, labels_ref, select_ref,
    send_lab, recv_lab, rolled, expanded, bias, proj, att, dqkv, cot, skip, back_src,
    scaled, scaled_in, low, low_in, part, part_in, summed, summed_in,
    local_s, halo_s, halo_r, lab_s, lab_r, skip_s, skip_r, back_s, back_r,
    sc_s, sc_r, low_s, low_r, pair_s, pair_r, grp_s, grp_r,
):
    ph, la, lo = lax.axis_index("phase"), lax.axis_index("lat"), lax.axis_index("lon")
    features = gain_ref.shape[-1]
    rows, cols = gq_ref.shape
    half = n_lon // 2
    chunks = cols // chunk
    par = lax.rem(lo, 2)
    grp = lo // 2

    def device(dlat, dlon):
        return (ph, lax.rem(la + dlat + n_lat, n_lat), lax.rem(lo + dlon + n_lon, n_lon))

    offsets = set()
    for dlat, dlon in ((0, 1), (1, 0), (1, 1)):
        offsets |= {(dlat % n_lat, dlon % n_lon), (-dlat % n_lat, -dlon % n_lon)}
    offsets |= {(d, 0) for d in range(1, n_lat)}
    offsets |= {(0, 2 * d) for d in range(1, half)}
    offsets = sorted(offsets)
    barrier = pltpu.get_barrier_semaphore()
    for dlat, dlon in offsets:
        pl.semaphore_signal(barrier, inc=1, device_id=device(dlat, dlon), device_id_type=MESH)
    pl.semaphore_signal(barrier, inc=1, device_id=(1 - ph, la, lo), device_id_type=MESH)

    def quadrant(ref, ih, jh):
        return ref.at[pl.ds(ih * LAT // 2, LAT // 2), pl.ds(jh * LON // 2, LON // 2)]

    loads = []
    for k, (src, dst) in enumerate((
        (labels_hbm, labels_ref),
        (table_hbm, table_ref),
        (select_hbm, select_ref),
        (quadrant(x_hbm, 1, 1), quadrant(win_x, 0, 0)),
        (quadrant(og_hbm, 1, 1), quadrant(win_og, 0, 0)),
        (gain_hbm, gain_ref),
        (wqkv_hbm, wqkv_ref),
        (wproj_hbm, wproj_ref),
    )):
        loads.append(pltpu.make_async_copy(src, dst, local_s.at[k]))
        loads[-1].start()
    loads[0].wait()
    lane = lax.broadcasted_iota(jnp.int32, (8, 128), 1)
    own_lab = jnp.zeros((8, 128), F32)
    for i in range(LAT):
        own_lab = jnp.where(lane == i, labels_ref[i].astype(F32), own_lab)
    send_lab[...] = own_lab

    pl.semaphore_wait(barrier, len(offsets) + 1)

    halo = []
    for ih, jh in ((0, 0), (0, 1), (1, 0)):
        for src, dst in ((x_hbm, win_x), (og_hbm, win_og)):
            k = len(halo)
            halo.append(pltpu.make_async_remote_copy(
                quadrant(src, ih, jh), quadrant(dst, 1 - ih, 1 - jh), halo_s.at[k], halo_r.at[k],
                device_id=device(ih - 1, jh - 1), device_id_type=MESH))
            halo[-1].start()
    lab_copy = pltpu.make_async_remote_copy(
        send_lab, recv_lab, lab_s.at[0], lab_r.at[0],
        device_id=device(-1, 0), device_id_type=MESH)
    lab_copy.start()
    for copy in loads[1:3]:
        copy.wait()

    table = table_ref[:, 128:512]
    for m in range(CELLS):
        i, j = divmod(m, LON)
        shift = (384 - (125 + 23 * i + j)) % 384
        rolled[8 * m:8 * m + 8, :] = pltpu.roll(table, shift, 1)[:, :128]
    wide = rolled[...]
    high = wide.astype(BF)
    rest = wide - high.astype(F32)
    mid = rest.astype(BF)
    least = (rest - mid.astype(F32)).astype(BF)
    column = select_ref[WROWS:WROWS + 128, :128].astype(BF)
    expanded[...] = (dot(high, column) + dot(mid, column)) + dot(least, column)

    lab_copy.wait()
    lab = jnp.where(lane < 3, recv_lab[...], own_lab)
    lab_row = dot(jnp.concatenate([lab, lab], axis=0).astype(BF), select_ref[WROWS + 128:WROWS + 256, :128].astype(BF))[0:1]
    lane1 = lax.broadcasted_iota(jnp.int32, (1, 128), 1)
    lab_row = jnp.where(lane1 < CELLS, lab_row, -1.0)
    row_id = lax.broadcasted_iota(jnp.int32, (ROWS, 128), 0)
    lane_id = lax.broadcasted_iota(jnp.int32, (ROWS, 128), 1)
    want = jnp.zeros((ROWS, 128), jnp.int32)
    for i in range(LAT):
        want = jnp.where(row_id >= LON * i, (i + 3) % 6, want)
    lab_col = jnp.sum(jnp.where(lane_id == want, lab[0:1], 0.0), axis=1, keepdims=True)
    row1 = lax.broadcasted_iota(jnp.int32, (ROWS, 1), 0)
    lab_col = jnp.where(row1 < CELLS, lab_col, -1.0)
    allowed = lab_col == lab_row
    for h in range(HEADS):
        one = expanded[pl.ds(h, CELLS, stride=8), :]
        one = jnp.concatenate([one, jnp.zeros((ROWS - CELLS, 128), F32)], axis=0)
        bias[h // 2, ROWS * (h % 2):ROWS * (h % 2 + 1), :] = jnp.where(allowed, one, MASKED)

    for copy in loads[3:] + halo:
        copy.wait()
    to_win = select_ref[:WROWS, :LEV * CELLS].astype(BF)
    x = dot(to_win, win_x[...].reshape(LEV * CELLS, features))
    og = dot(to_win, win_og[...].reshape(LEV * CELLS, features))
    gain = gain_ref[...]
    center = jnp.mean(x, axis=-1, keepdims=True)
    spread = jnp.mean(jnp.square(x - center), axis=-1, keepdims=True)
    inv_std = lax.rsqrt(spread + EPSILON)
    normed = (x - center) * inv_std
    scaled[...] = (normed * gain).astype(BF)
    sc_copies = []
    for d in range(1, n_lat):
        sc_copies.append(pltpu.make_async_remote_copy(
            scaled, scaled_in.at[d - 1], sc_s.at[d - 1], sc_r.at[d - 1],
            device_id=device(d, 0), device_id_type=MESH))
        sc_copies[-1].start()
    proj[...] = dot(scaled[...], wqkv_ref[...], NT).astype(BF)
    first_half = lax.broadcasted_iota(jnp.int32, (ROWS, 128), 1) < 64
    zero = jnp.zeros((ROWS, 128), BF)

    def both(pair):
        return jnp.concatenate(
            [jnp.where(first_half, pair, zero), jnp.where(first_half, zero, pair)], axis=0)

    def query_pair(p, hp):
        pair = proj[ROWS * p:ROWS * (p + 1), 128 * hp:128 * (hp + 1)]
        return both(pair * jnp.asarray(0.125, BF))

    def later_pair(which, p, hp):
        start = features * which + 128 * hp
        return proj[ROWS * p:ROWS * (p + 1), start:start + 128]

    for p in range(LEV):
        for hp in range(HEADS // 2):
            scores = dot(query_pair(p, hp), later_pair(1, p, hp), NT) + bias[hp][:, :ROWS]
            weights = jnp.exp(scores - jnp.max(scores, axis=-1, keepdims=True))
            att[4 * p + hp] = weights / jnp.sum(weights, axis=-1, keepdims=True)

    def backprop(p, cotangent, accumulate):
        d_attended = dot(cotangent, wproj_ref[...]).astype(BF)
        own = slice(ROWS * p, ROWS * (p + 1))
        parts = [[], [], []]
        for hp in range(HEADS // 2):
            d_pair = both(d_attended[:, 128 * hp:128 * (hp + 1)])
            attention = att[4 * p + hp]
            d_probs = dot(d_pair, later_pair(2, p, hp), NT)
            d_value = dot(attention.astype(BF), d_pair, TN)
            inner = jnp.sum(attention * d_probs, axis=-1, keepdims=True)
            d_scores = (attention * (d_probs - inner)).astype(BF)
            d_both = dot(d_scores, later_pair(1, p, hp))
            d_query = jnp.where(first_half, d_both[:ROWS], d_both[ROWS:]) * 0.125
            d_key = dot(d_scores, query_pair(p, hp), TN)
            for which, value in enumerate((d_query, d_key, d_value)):
                start = features * which + 128 * hp
                parts[which].append(value.astype(BF))
                at = (own, slice(start, start + 128))
                dqkv[at] = dqkv[at] + value if accumulate else value
        d_low = jnp.concatenate(parts[0] + parts[1] + parts[2], axis=1)
        d_normed = dot(d_low, wqkv_ref[...]) * gain
        return inv_std[own] * (
            d_normed
            - jnp.mean(d_normed, axis=-1, keepdims=True)
            - normed[own] * jnp.mean(d_normed * normed[own], axis=-1, keepdims=True))

    totals, skips = [], []
    for p in range(LEV):
        og_p = og[ROWS * p:ROWS * (p + 1)]
        totals.append(og_p + backprop(p, og_p.astype(BF), False))
        cot[p] = totals[p].astype(BF)
        skips.append(pltpu.make_async_remote_copy(
            cot.at[p], skip.at[p], skip_s.at[p], skip_r.at[p],
            device_id=(1 - ph, la, lo), device_id_type=MESH))
        pl.when(ph == 1)(skips[p].start)

    @pl.when(ph == 0)
    def _():
        for p in range(LEV):
            skips[p].wait_recv()
            received = skip[p]
            second = backprop(p, received, True)
            cot[p] = (totals[p] + (received.astype(F32) + second)).astype(BF)

    for l in range(n_lat):
        low[l] = dqkv[:, cols * l:cols * (l + 1)].astype(BF)
    low_copies = []
    for d in range(1, n_lat):
        to = device(d, 0)
        low_copies.append(pltpu.make_async_remote_copy(
            low.at[to[1]], low_in.at[d - 1], low_s.at[d - 1], low_r.at[d - 1],
            device_id=to, device_id_type=MESH))
        low_copies[-1].start()

    whole = cot[...].reshape(WROWS, features)
    back_src[...] = dot(to_win, whole, TN).astype(BF).reshape(LAT, LON, LEV, features)
    back = []
    for ih, jh in ((0, 0), (0, 1), (1, 0)):
        k = len(back)
        back.append(pltpu.make_async_remote_copy(
            quadrant(back_src, 1 - ih, 1 - jh), quadrant(gin_ref, ih, jh), back_s.at[k], back_r.at[k],
            device_id=device(1 - ih, 1 - jh), device_id_type=MESH))
    gin_ref[LAT // 2:, LON // 2:] = back_src[:LAT // 2, :LON // 2]

    for copy in sc_copies + low_copies:
        copy.wait()
    pair_to = (ph, la, lo + 1 - 2 * par)
    pairs = []
    for c in range(chunks):
        at = slice(chunk * c, chunk * (c + 1))
        value = dot(scaled[...], low[la][:, at], TN)
        for d in range(1, n_lat):
            value = value + dot(scaled_in[d - 1], low_in[d - 1][:, at], TN)
        value = value.astype(BF)
        for j in range(n_lon):
            part[c, j % 2, j // 2] = value[rows * j:rows * (j + 1)]
        pairs.append(pltpu.make_async_remote_copy(
            part.at[c, 1 - par], part_in.at[c], pair_s.at[c], pair_r.at[c],
            device_id=pair_to, device_id_type=MESH))
        pairs[-1].start()
    for copy in back:
        copy.start()
    groups = []
    for c in range(chunks):
        pairs[c].wait_recv()
        summed[c] = (part[c, par].astype(F32) + part_in[c].astype(F32)).astype(BF)
        for d in range(1, half):
            to = lax.rem(grp + d, half)
            groups.append(pltpu.make_async_remote_copy(
                summed.at[c, to], summed_in.at[c, d - 1],
                grp_s.at[c, d - 1], grp_r.at[c, d - 1],
                device_id=(ph, la, 2 * to + par), device_id_type=MESH))
            groups[-1].start()

    for copy in groups:
        copy.wait()
    for c in range(chunks):
        value = summed[c, grp].astype(F32)
        for d in range(1, half):
            value = value + summed_in[c, d - 1].astype(F32)
        gq_ref[:, chunk * c:chunk * (c + 1)] = value
    for copy in pairs:
        copy.wait_send()
    for copy in back:
        copy.wait()

    @pl.when(ph == 1)
    def _():
        for copy in skips:
            copy.wait_send()


def cells_first(field):
    return field[0].transpose(1, 2, 0, 3)


def per_device(n_lat, n_lon, x_in, out_grad, w_qkv, w_proj, norm_gain, bias_table, lat_labels):
    features = x_in.shape[-1]
    outs = w_qkv.shape[1]
    cols, rows = outs // n_lat, features // n_lon
    chunk = 256 if cols % 256 == 0 else cols
    chunks, half = cols // chunk, n_lon // 2
    vmem = pl.BlockSpec(memory_space=pltpu.VMEM)
    dma = lambda *shape: pltpu.SemaphoreType.DMA(shape)
    peers = max(n_lat - 1, 1)
    grid = (LAT, LON, LEV, features)
    grad_input, grad_qkv = pl.pallas_call(
        functools.partial(kernel, n_lat, n_lon, chunk),
        out_shape=(
            jax.ShapeDtypeStruct(grid, BF),
            jax.ShapeDtypeStruct((rows, cols), F32),
        ),
        in_specs=[pl.BlockSpec(memory_space=pl.ANY)] * 8,
        out_specs=(vmem, vmem),
        scratch_shapes=[
            pltpu.VMEM(grid, BF),
            pltpu.VMEM(grid, BF),
            pltpu.VMEM((outs, features), BF),
            pltpu.VMEM((features, features), BF),
            pltpu.VMEM((1, features), F32),
            pltpu.VMEM(bias_table.shape[1:], F32),
            pltpu.SMEM((LAT,), jnp.int32),
            pltpu.VMEM((WROWS + 256, 256), F32),
            pltpu.VMEM((8, 128), F32),
            pltpu.VMEM((8, 128), F32),
            pltpu.VMEM((8 * CELLS, 128), F32),
            pltpu.VMEM((8 * CELLS, 128), F32),
            pltpu.VMEM((HEADS // 2, 2 * ROWS, 128), F32),
            pltpu.VMEM((WROWS, outs), BF),
            pltpu.VMEM((HEADS, 2 * ROWS, ROWS), F32),
            pltpu.VMEM((WROWS, outs), F32),
            pltpu.VMEM((LEV, ROWS, features), BF),
            pltpu.VMEM((LEV, ROWS, features), BF),
            pltpu.VMEM(grid, BF),
            pltpu.VMEM((WROWS, features), BF),
            pltpu.VMEM((peers, WROWS, features), BF),
            pltpu.VMEM((n_lat, WROWS, cols), BF),
            pltpu.VMEM((peers, WROWS, cols), BF),
            pltpu.VMEM((chunks, 2, half, rows, chunk), BF),
            pltpu.VMEM((chunks, half, rows, chunk), BF),
            pltpu.VMEM((chunks, half, rows, chunk), BF),
            pltpu.VMEM((chunks, half - 1, rows, chunk), BF),
            dma(8), dma(6), dma(6), dma(1), dma(1), dma(LEV), dma(LEV), dma(3), dma(3),
            dma(peers), dma(peers), dma(peers), dma(peers),
            dma(chunks), dma(chunks), dma(chunks, half - 1), dma(chunks, half - 1),
        ],
        compiler_params=pltpu.CompilerParams(
            collective_id=0, has_side_effects=True, vmem_limit_bytes=60 * 1024 * 1024),
    )(
        cells_first(x_in), cells_first(out_grad), w_qkv[0], w_proj[0], norm_gain,
        bias_table[0], lat_labels, jnp.asarray(selections()))
    return grad_input.transpose(2, 0, 1, 3)[None], grad_qkv.T[None]


def solution(mesh):
    in_specs = (
        P("phase", None, "lat", "lon", None),
        P("phase", None, "lat", "lon", None),
        P("phase", None, None),
        P("phase", None, None),
        P("phase", None),
        P("phase", None, None),
        P("lat"),
    )
    out_specs = (P("phase", None, "lat", "lon", None), P("phase", "lat", "lon"))
    return jax.shard_map(
        functools.partial(per_device, mesh.shape["lat"], mesh.shape["lon"]),
        mesh=mesh, in_specs=in_specs, out_specs=out_specs, check_vma=False)
```

time: 58.5 us -> 45.5 us (0.78)
  local copies, waits for them, and re-layouts: 13.1 us -> 3.29 us
  Pallas kernels: 44.1 us -> 41.4 us
    unnamed x26 -> x2, local copies, waits for them, and re-layouts: 13.1 us -> 3.29 us
    pallas_call x1, Pallas kernels: 44.1 us -> 41.4 us  [per_device(): pl.pallas_call(functools.partial(kernel, n_lat, n_lon, chunk), out_shape=...]
where the time goes in v2:
time: 45.5 us; the launch traced here: 45.3 us
  Pallas kernels  41.4 us (91%)
  local copies, waits for them, and re-layouts  3.29 us (7%)
  between operations  0.64 us (1%)
    pallas_call x1, Pallas kernels, per_device(): pl.pallas_call(functools.partial(kernel, n_lat, n_lon, chunk), out_shape=...  41.4 us
    unnamed x2, local copies, waits for them, and re-layouts  3.29 us

profile of v2, /device:TPU:0, one launch (start us, length us, event | category | flops | bytes accessed | tf_op | source)
XLA Modules:
  0.0 45.3 jit_solution(1664890823979682693)
XLA Ops:
  0.6 41.4 %shard_map.95 = (bf16[6,12,2,512]{3,2,1,0:T(2,128)(2,1)}, f32[64,768]{1,0:T(8,128)}) custom-call(bf16[6,12,2,512]{3,2,1,0:T(2,128)(2,1)} %bitcast.19, bf16[6,12,2,512]{3,2,1,0:T(2,128)(2,1)} %bitcast.20, bf16[1536,512]{1,0:T(8,128)(2,1)} %bitcast.15, bf16[512,512]{1,0:T(8,128)(2,1)} %bitcast.16, f32[1,512]{1,0:T(1,128)} %gain_hbm.1, f32[8,759]{1,0:T(8,128)} %bitcast.21, ...), custom_call_target="tpu_custom_call" | custom-call | tf_op jit(solution)/shard_map/pallas_call | solution.py:312
  42.0 1.7 %copy.12 = bf16[1,2,6,12,512]{4,1,3,2,0:T(2,128)(2,1)} copy(bf16[1,2,6,12,512]{4,1,3,2,0:T(2,128)(2,1)} %bitcast.18) | data formatting | bytes 294912
  43.7 1.6 %copy.13 = f32[1,768,64]{1,2,0:T(8,128)} copy(f32[1,768,64]{1,2,0:T(8,128)} %bitcast.17) | data formatting | bytes 393216

commit v3 on v2

--- a/solution.py
+++ b/solution.py
@@ -32,6 +32,21 @@
     return packed
 
 
+def steps(features, cols, chunk, n_lat):
+    order, last = [], []
+    for l in range(n_lat):
+        starts = range(cols * l, cols * (l + 1), chunk)
+        pair = {
+            start: max(c % features for c in range(start, start + chunk, 64)) // 128
+            for start in starts
+        }
+        order.append(sorted(starts, key=lambda start: pair[start]))
+        last.append([pair[start] for start in order[-1]])
+    if chunk != 128:
+        return order, [HEADS // 2 - 1] * (cols // chunk)
+    return order, [max(step) for step in zip(*last)]
+
+
 def dot(a, b, dims=((1,), (0,))):
     return lax.dot_general(a, b, (dims, ((), ())), preferred_element_type=F32)
 
@@ -41,12 +56,12 @@
 
 
 def kernel(
-    n_lat, n_lon, chunk,
+    n_lat, n_lon, chunk, order, ready,
     x_hbm, og_hbm, wqkv_hbm, wproj_hbm, gain_hbm, table_hbm, labels_hbm, select_hbm,
     gin_ref, gq_ref,
     win_x, win_og, wqkv_ref, wproj_ref, gain_ref, table_ref, labels_ref, select_ref,
     send_lab, recv_lab, rolled, expanded, bias, proj, att, dqkv, cot, skip, back_src,
-    scaled, scaled_in, low, low_in, part, part_in, summed, summed_in,
+    scaled, scaled_in, turned, low, low_in, part, part_in, summed, summed_in,
     local_s, halo_s, halo_r, lab_s, lab_r, skip_s, skip_r, back_s, back_r,
     sc_s, sc_r, low_s, low_r, pair_s, pair_r, grp_s, grp_r,
 ):
@@ -183,26 +198,28 @@
             weights = jnp.exp(scores - jnp.max(scores, axis=-1, keepdims=True))
             att[4 * p + hp] = weights / jnp.sum(weights, axis=-1, keepdims=True)
 
-    def backprop(p, cotangent, accumulate):
-        d_attended = dot(cotangent, wproj_ref[...]).astype(BF)
+    def attended_grad(p, cotangent):
+        return dot(cotangent, wproj_ref[...]).astype(BF)
+
+    def attention_grad(p, hp, d_attended, accumulate):
+        d_pair = both(d_attended[:, 128 * hp:128 * (hp + 1)])
+        attention = att[4 * p + hp]
+        d_probs = dot(d_pair, later_pair(2, p, hp), NT)
+        d_value = dot(attention.astype(BF), d_pair, TN)
+        inner = jnp.sum(attention * d_probs, axis=-1, keepdims=True)
+        d_scores = (attention * (d_probs - inner)).astype(BF)
+        d_both = dot(d_scores, later_pair(1, p, hp))
+        d_query = jnp.where(first_half, d_both[:ROWS], d_both[ROWS:]) * 0.125
+        d_key = dot(d_scores, query_pair(p, hp), TN)
+        for which, value in enumerate((d_query, d_key, d_value)):
+            start = features * which + 128 * hp
+            at = (slice(ROWS * p, ROWS * (p + 1)), slice(start, start + 128))
+            dqkv[at] = dqkv[at] + value if accumulate else value
+        return [value.astype(BF) for value in (d_query, d_key, d_value)]
+
+    def input_grad(p, parts):
         own = slice(ROWS * p, ROWS * (p + 1))
-        parts = [[], [], []]
-        for hp in range(HEADS // 2):
-            d_pair = both(d_attended[:, 128 * hp:128 * (hp + 1)])
-            attention = att[4 * p + hp]
-            d_probs = dot(d_pair, later_pair(2, p, hp), NT)
-            d_value = dot(attention.astype(BF), d_pair, TN)
-            inner = jnp.sum(attention * d_probs, axis=-1, keepdims=True)
-            d_scores = (attention * (d_probs - inner)).astype(BF)
-            d_both = dot(d_scores, later_pair(1, p, hp))
-            d_query = jnp.where(first_half, d_both[:ROWS], d_both[ROWS:]) * 0.125
-            d_key = dot(d_scores, query_pair(p, hp), TN)
-            for which, value in enumerate((d_query, d_key, d_value)):
-                start = features * which + 128 * hp
-                parts[which].append(value.astype(BF))
-                at = (own, slice(start, start + 128))
-                dqkv[at] = dqkv[at] + value if accumulate else value
-        d_low = jnp.concatenate(parts[0] + parts[1] + parts[2], axis=1)
+        d_low = jnp.concatenate([pair[w] for w in range(3) for pair in parts], axis=1)
         d_normed = dot(d_low, wqkv_ref[...]) * gain
         return inv_std[own] * (
             d_normed
@@ -212,30 +229,77 @@
     totals, skips = [], []
     for p in range(LEV):
         og_p = og[ROWS * p:ROWS * (p + 1)]
-        totals.append(og_p + backprop(p, og_p.astype(BF), False))
+        d_attended = attended_grad(p, og_p.astype(BF))
+        parts = [attention_grad(p, hp, d_attended, False) for hp in range(HEADS // 2)]
+        totals.append(og_p + input_grad(p, parts))
         cot[p] = totals[p].astype(BF)
         skips.append(pltpu.make_async_remote_copy(
             cot.at[p], skip.at[p], skip_s.at[p], skip_r.at[p],
             device_id=(1 - ph, la, lo), device_id_type=MESH))
         pl.when(ph == 1)(skips[p].start)
 
+    turned[0] = scaled[...].T
+    for d in range(1, n_lat):
+        sc_copies[d - 1].wait()
+        turned[d] = scaled_in[d - 1].T
+    low_copies, pairs = [], []
+    for c in range(chunks):
+        low_copies.append([])
+        for d in range(1, n_lat):
+            to = device(d, 0)
+            low_copies[c].append(pltpu.make_async_remote_copy(
+                low.at[to[1], c], low_in.at[d - 1, c], low_s.at[d - 1, c], low_r.at[d - 1, c],
+                device_id=to, device_id_type=MESH))
+        pairs.append(pltpu.make_async_remote_copy(
+            part.at[c, 1 - par], part_in.at[c], pair_s.at[c], pair_r.at[c],
+            device_id=(ph, la, lo + 1 - 2 * par), device_id_type=MESH))
+
+    def send_factors(c):
+        for l in range(n_lat):
+            low[l, c] = dqkv[:, order[l][c]:order[l][c] + chunk].astype(BF)
+        for copy in low_copies[c]:
+            copy.start()
+
+    def send_sums(c):
+        for copy in low_copies[c]:
+            copy.wait_recv()
+        value = dot(turned[0], low[la, c])
+        for d in range(1, n_lat):
+            value = value + dot(turned[d], low_in[d - 1, c])
+        value = value.astype(BF)
+        for j in range(n_lon):
+            part[c, j % 2, j // 2] = value[rows * j:rows * (j + 1)]
+        pairs[c].start()
+
+    @pl.when(ph == 1)
+    def _():
+        for c in range(chunks):
+            send_factors(c)
+        for c in range(chunks):
+            send_sums(c)
+
     @pl.when(ph == 0)
     def _():
+        skips[0].wait_recv()
+        d_attended = attended_grad(0, skip[0])
+        all_parts = [[attention_grad(0, hp, d_attended, True) for hp in range(HEADS // 2)], []]
+        skips[1].wait_recv()
+        d_attended = attended_grad(1, skip[1])
+        sent = 0
+        for hp in range(HEADS // 2):
+            all_parts[1].append(attention_grad(1, hp, d_attended, True))
+            due = [c for c in range(chunks) if ready[c] == hp]
+            for c in due:
+                send_factors(c)
+            while due and sent < due[0]:
+                send_sums(sent)
+                sent += 1
+        while sent < chunks:
+            send_sums(sent)
+            sent += 1
         for p in range(LEV):
-            skips[p].wait_recv()
-            received = skip[p]
-            second = backprop(p, received, True)
-            cot[p] = (totals[p] + (received.astype(F32) + second)).astype(BF)
-
-    for l in range(n_lat):
-        low[l] = dqkv[:, cols * l:cols * (l + 1)].astype(BF)
-    low_copies = []
-    for d in range(1, n_lat):
-        to = device(d, 0)
-        low_copies.append(pltpu.make_async_remote_copy(
-            low.at[to[1]], low_in.at[d - 1], low_s.at[d - 1], low_r.at[d - 1],
-            device_id=to, device_id_type=MESH))
-        low_copies[-1].start()
+            second = input_grad(p, all_parts[p])
+            cot[p] = (totals[p] + (skip[p].astype(F32) + second)).astype(BF)
 
     whole = cot[...].reshape(WROWS, features)
     back_src[...] = dot(to_win, whole, TN).astype(BF).reshape(LAT, LON, LEV, features)
@@ -247,22 +311,6 @@
             device_id=device(1 - ih, 1 - jh), device_id_type=MESH))
     gin_ref[LAT // 2:, LON // 2:] = back_src[:LAT // 2, :LON // 2]
 
-    for copy in sc_copies + low_copies:
-        copy.wait()
-    pair_to = (ph, la, lo + 1 - 2 * par)
-    pairs = []
-    for c in range(chunks):
-        at = slice(chunk * c, chunk * (c + 1))
-        value = dot(scaled[...], low[la][:, at], TN)
-        for d in range(1, n_lat):
-            value = value + dot(scaled_in[d - 1], low_in[d - 1][:, at], TN)
-        value = value.astype(BF)
-        for j in range(n_lon):
-            part[c, j % 2, j // 2] = value[rows * j:rows * (j + 1)]
-        pairs.append(pltpu.make_async_remote_copy(
-            part.at[c, 1 - par], part_in.at[c], pair_s.at[c], pair_r.at[c],
-            device_id=pair_to, device_id_type=MESH))
-        pairs[-1].start()
     for copy in back:
         copy.start()
     groups = []
@@ -277,14 +325,21 @@
                 device_id=(ph, la, 2 * to + par), device_id_type=MESH))
             groups[-1].start()
 
-    for copy in groups:
-        copy.wait()
     for c in range(chunks):
         value = summed[c, grp].astype(F32)
         for d in range(1, half):
+            groups[c * (half - 1) + d - 1].wait_recv()
             value = value + summed_in[c, d - 1].astype(F32)
-        gq_ref[:, chunk * c:chunk * (c + 1)] = value
-    for copy in pairs:
+        for l in range(n_lat):
+            at = slice(order[l][c] - cols * l, order[l][c] - cols * l + chunk)
+
+            @pl.when(la == l)
+            def _(value=value, at=at):
+                gq_ref[:, at] = value
+
+    for copy in groups:
+        copy.wait_send()
+    for copy in pairs + [copy for step in low_copies for copy in step]:
         copy.wait_send()
     for copy in back:
         copy.wait()
@@ -299,18 +354,30 @@
     return field[0].transpose(1, 2, 0, 3)
 
 
+def finish(gin_hbm, gq_hbm, gin_out, gq_out, sems):
+    copies = [
+        pltpu.make_async_copy(gin_hbm, gin_out, sems.at[0]),
+        pltpu.make_async_copy(gq_hbm, gq_out, sems.at[1]),
+    ]
+    for copy in copies:
+        copy.start()
+    for copy in copies:
+        copy.wait()
+
+
 def per_device(n_lat, n_lon, x_in, out_grad, w_qkv, w_proj, norm_gain, bias_table, lat_labels):
     features = x_in.shape[-1]
     outs = w_qkv.shape[1]
     cols, rows = outs // n_lat, features // n_lon
-    chunk = 256 if cols % 256 == 0 else cols
+    chunk = 128 if cols % 128 == 0 else cols
     chunks, half = cols // chunk, n_lon // 2
+    order, ready = steps(features, cols, chunk, n_lat)
     vmem = pl.BlockSpec(memory_space=pltpu.VMEM)
     dma = lambda *shape: pltpu.SemaphoreType.DMA(shape)
     peers = max(n_lat - 1, 1)
     grid = (LAT, LON, LEV, features)
     grad_input, grad_qkv = pl.pallas_call(
-        functools.partial(kernel, n_lat, n_lon, chunk),
+        functools.partial(kernel, n_lat, n_lon, chunk, order, ready),
         out_shape=(
             jax.ShapeDtypeStruct(grid, BF),
             jax.ShapeDtypeStruct((rows, cols), F32),
@@ -339,14 +406,15 @@
             pltpu.VMEM(grid, BF),
             pltpu.VMEM((WROWS, features), BF),
             pltpu.VMEM((peers, WROWS, features), BF),
-            pltpu.VMEM((n_lat, WROWS, cols), BF),
-            pltpu.VMEM((peers, WROWS, cols), BF),
+            pltpu.VMEM((n_lat, features, WROWS), BF),
+            pltpu.VMEM((n_lat, chunks, WROWS, chunk), BF),
+            pltpu.VMEM((peers, chunks, WROWS, chunk), BF),
             pltpu.VMEM((chunks, 2, half, rows, chunk), BF),
             pltpu.VMEM((chunks, half, rows, chunk), BF),
             pltpu.VMEM((chunks, half, rows, chunk), BF),
             pltpu.VMEM((chunks, half - 1, rows, chunk), BF),
             dma(8), dma(6), dma(6), dma(1), dma(1), dma(LEV), dma(LEV), dma(3), dma(3),
-            dma(peers), dma(peers), dma(peers), dma(peers),
+            dma(peers), dma(peers), dma(peers, chunks), dma(peers, chunks),
             dma(chunks), dma(chunks), dma(chunks, half - 1), dma(chunks, half - 1),
         ],
         compiler_params=pltpu.CompilerParams(
@@ -354,6 +422,16 @@
     )(
         cells_first(x_in), cells_first(out_grad), w_qkv[0], w_proj[0], norm_gain,
         bias_table[0], lat_labels, jnp.asarray(selections()))
+    grad_input, grad_qkv = pl.pallas_call(
+        finish,
+        out_shape=(
+            jax.ShapeDtypeStruct(grid, BF),
+            jax.ShapeDtypeStruct((rows, cols), F32),
+        ),
+        in_specs=[pl.BlockSpec(memory_space=pl.ANY)] * 2,
+        out_specs=[pl.BlockSpec(memory_space=pl.ANY)] * 2,
+        scratch_shapes=[pltpu.SemaphoreType.DMA((2,))],
+    )(grad_input, grad_qkv)
     return grad_input.transpose(2, 0, 1, 3)[None], grad_qkv.T[None]
 
 

time: 45.5 us -> 52.7 us (1.16)
  Pallas kernels: 41.4 us -> 51.9 us
  local copies, waits for them, and re-layouts: 3.29 us -> 0 us
    pallas_call x1 -> x2, Pallas kernels: 41.4 us -> 51.9 us  [the longest x1 40.4 us: per_device(): pl.pallas_call(functools.partial(kernel, n_lat, n_lon, chunk, order, read...]
    unnamed x2 -> x0, local copies, waits for them, and re-layouts: 3.29 us -> none
where the time goes in v3:
time: 52.7 us; the launch traced here: 52.6 us
  Pallas kernels  51.9 us (98%)
  between operations  0.64 us (1%)
    pallas_call x1, Pallas kernels, per_device(): pl.pallas_call(functools.partial(kernel, n_lat, n_lon, chunk, order, read...  40.4 us
    pallas_call x1, Pallas kernels, per_device(): pl.pallas_call(finish, out_shape=(jax.ShapeDtypeStruct(grid, BF), jax.Sha...  11.5 us

profile of v3, /device:TPU:0, one launch (start us, length us, event | category | flops | bytes accessed | tf_op | source)
XLA Modules:
  0.0 52.6 jit_solution(314982993842279033)
XLA Ops:
  0.6 40.4 %shard_map.95 = (bf16[6,12,2,512]{3,2,1,0:T(2,128)(2,1)}, f32[64,768]{1,0:T(8,128)}) custom-call(bf16[6,12,2,512]{3,2,1,0:T(2,128)(2,1)} %bitcast.17, bf16[6,12,2,512]{3,2,1,0:T(2,128)(2,1)} %bitcast.18, bf16[1536,512]{1,0:T(8,128)(2,1)} %bitcast.15, bf16[512,512]{1,0:T(8,128)(2,1)} %bitcast.16, f32[1,512]{1,0:T(1,128)} %gain_hbm.1, f32[8,759]{1,0:T(8,128)} %bitcast.19, ...), custom_call_target="tpu_custom_call" | custom-call | tf_op jit(solution)/shard_map/pallas_call | solution.py:379
  41.0 11.5 %shard_map.96 = (bf16[6,12,2,512]{3,2,1,0:T(2,128)(2,1)}, f32[64,768]{1,0:T(8,128)}) custom-call(bf16[6,12,2,512]{3,2,1,0:T(2,128)(2,1)} %get-tuple-element.6.gin_hbm, f32[64,768]{1,0:T(8,128)} %get-tuple-element.7.gq_hbm), custom_call_target="tpu_custom_call" | custom-call | tf_op jit(solution)/shard_map/pallas_call | solution.py:425

commit v4 on v3

--- a/solution.py
+++ b/solution.py
@@ -32,21 +32,6 @@
     return packed
 
 
-def steps(features, cols, chunk, n_lat):
-    order, last = [], []
-    for l in range(n_lat):
-        starts = range(cols * l, cols * (l + 1), chunk)
-        pair = {
-            start: max(c % features for c in range(start, start + chunk, 64)) // 128
-            for start in starts
-        }
-        order.append(sorted(starts, key=lambda start: pair[start]))
-        last.append([pair[start] for start in order[-1]])
-    if chunk != 128:
-        return order, [HEADS // 2 - 1] * (cols // chunk)
-    return order, [max(step) for step in zip(*last)]
-
-
 def dot(a, b, dims=((1,), (0,))):
     return lax.dot_general(a, b, (dims, ((), ())), preferred_element_type=F32)
 
@@ -56,7 +41,7 @@
 
 
 def kernel(
-    n_lat, n_lon, chunk, order, ready,
+    n_lat, n_lon, chunk,
     x_hbm, og_hbm, wqkv_hbm, wproj_hbm, gain_hbm, table_hbm, labels_hbm, select_hbm,
     gin_ref, gq_ref,
     win_x, win_og, wqkv_ref, wproj_ref, gain_ref, table_ref, labels_ref, select_ref,
@@ -192,35 +177,38 @@
         start = features * which + 128 * hp
         return proj[ROWS * p:ROWS * (p + 1), start:start + 128]
 
-    for p in range(LEV):
-        for hp in range(HEADS // 2):
-            scores = dot(query_pair(p, hp), later_pair(1, p, hp), NT) + bias[hp][:, :ROWS]
-            weights = jnp.exp(scores - jnp.max(scores, axis=-1, keepdims=True))
-            att[4 * p + hp] = weights / jnp.sum(weights, axis=-1, keepdims=True)
+    pairs_of = range(HEADS // 2)
+    units = [(p, hp) for p in range(LEV) for hp in pairs_of]
+    scores = [
+        dot(query_pair(p, hp), later_pair(1, p, hp), NT) + bias[hp][:, :ROWS] for p, hp in units]
+    weights = [jnp.exp(s - jnp.max(s, axis=-1, keepdims=True)) for s in scores]
+    scales = [1.0 / jnp.sum(w, axis=-1, keepdims=True) for w in weights]
+    for k, (w, scale) in enumerate(zip(weights, scales)):
+        att[k] = w * scale
 
     def attended_grad(p, cotangent):
         return dot(cotangent, wproj_ref[...]).astype(BF)
 
-    def attention_grad(p, hp, d_attended, accumulate):
-        d_pair = both(d_attended[:, 128 * hp:128 * (hp + 1)])
-        attention = att[4 * p + hp]
-        d_probs = dot(d_pair, later_pair(2, p, hp), NT)
-        d_value = dot(attention.astype(BF), d_pair, TN)
-        inner = jnp.sum(attention * d_probs, axis=-1, keepdims=True)
-        d_scores = (attention * (d_probs - inner)).astype(BF)
-        d_both = dot(d_scores, later_pair(1, p, hp))
-        d_query = jnp.where(first_half, d_both[:ROWS], d_both[ROWS:]) * 0.125
-        d_key = dot(d_scores, query_pair(p, hp), TN)
-        for which, value in enumerate((d_query, d_key, d_value)):
-            start = features * which + 128 * hp
-            at = (slice(ROWS * p, ROWS * (p + 1)), slice(start, start + 128))
+    def attention_grad(p, d_attended, accumulate):
+        d_pairs = [both(d_attended[:, 128 * hp:128 * (hp + 1)]) for hp in pairs_of]
+        d_probs = [dot(d_pairs[hp], later_pair(2, p, hp), NT) for hp in pairs_of]
+        d_values = [dot(att[4 * p + hp].astype(BF), d_pairs[hp], TN) for hp in pairs_of]
+        inner = [
+            jnp.sum(att[4 * p + hp] * d_probs[hp], axis=-1, keepdims=True) for hp in pairs_of]
+        d_scores = [
+            (att[4 * p + hp] * (d_probs[hp] - inner[hp])).astype(BF) for hp in pairs_of]
+        d_both = [dot(d_scores[hp], later_pair(1, p, hp)) for hp in pairs_of]
+        d_keys = [dot(d_scores[hp], query_pair(p, hp), TN) for hp in pairs_of]
+        d_queries = [jnp.where(first_half, d[:ROWS], d[ROWS:]) * 0.125 for d in d_both]
+        values = d_queries + d_keys + d_values
+        for k, value in enumerate(values):
+            at = (slice(ROWS * p, ROWS * (p + 1)), slice(128 * k, 128 * (k + 1)))
             dqkv[at] = dqkv[at] + value if accumulate else value
-        return [value.astype(BF) for value in (d_query, d_key, d_value)]
-
-    def input_grad(p, parts):
+        return [value.astype(BF) for value in values]
+
+    def input_grad(p, lows):
         own = slice(ROWS * p, ROWS * (p + 1))
-        d_low = jnp.concatenate([pair[w] for w in range(3) for pair in parts], axis=1)
-        d_normed = dot(d_low, wqkv_ref[...]) * gain
+        d_normed = dot(jnp.concatenate(lows, axis=1), wqkv_ref[...]) * gain
         return inv_std[own] * (
             d_normed
             - jnp.mean(d_normed, axis=-1, keepdims=True)
@@ -230,8 +218,7 @@
     for p in range(LEV):
         og_p = og[ROWS * p:ROWS * (p + 1)]
         d_attended = attended_grad(p, og_p.astype(BF))
-        parts = [attention_grad(p, hp, d_attended, False) for hp in range(HEADS // 2)]
-        totals.append(og_p + input_grad(p, parts))
+        totals.append(og_p + input_grad(p, attention_grad(p, d_attended, False)))
         cot[p] = totals[p].astype(BF)
         skips.append(pltpu.make_async_remote_copy(
             cot.at[p], skip.at[p], skip_s.at[p], skip_r.at[p],
@@ -256,7 +243,8 @@
 
     def send_factors(c):
         for l in range(n_lat):
-            low[l, c] = dqkv[:, order[l][c]:order[l][c] + chunk].astype(BF)
+            start = cols * l + chunk * c
+            low[l, c] = dqkv[:, start:start + chunk].astype(BF)
         for copy in low_copies[c]:
             copy.start()
 
@@ -282,23 +270,16 @@
     def _():
         skips[0].wait_recv()
         d_attended = attended_grad(0, skip[0])
-        all_parts = [[attention_grad(0, hp, d_attended, True) for hp in range(HEADS // 2)], []]
+        all_lows = [attention_grad(0, d_attended, True)]
         skips[1].wait_recv()
         d_attended = attended_grad(1, skip[1])
-        sent = 0
-        for hp in range(HEADS // 2):
-            all_parts[1].append(attention_grad(1, hp, d_attended, True))
-            due = [c for c in range(chunks) if ready[c] == hp]
-            for c in due:
-                send_factors(c)
-            while due and sent < due[0]:
-                send_sums(sent)
-                sent += 1
-        while sent < chunks:
-            send_sums(sent)
-            sent += 1
+        all_lows.append(attention_grad(1, d_attended, True))
+        for c in range(chunks):
+            send_factors(c)
+        for c in range(chunks):
+            send_sums(c)
         for p in range(LEV):
-            second = input_grad(p, all_parts[p])
+            second = input_grad(p, all_lows[p])
             cot[p] = (totals[p] + (skip[p].astype(F32) + second)).astype(BF)
 
     whole = cot[...].reshape(WROWS, features)
@@ -330,12 +311,7 @@
         for d in range(1, half):
             groups[c * (half - 1) + d - 1].wait_recv()
             value = value + summed_in[c, d - 1].astype(F32)
-        for l in range(n_lat):
-            at = slice(order[l][c] - cols * l, order[l][c] - cols * l + chunk)
-
-            @pl.when(la == l)
-            def _(value=value, at=at):
-                gq_ref[:, at] = value
+        gq_ref[:, chunk * c:chunk * (c + 1)] = value
 
     for copy in groups:
         copy.wait_send()
@@ -354,15 +330,23 @@
     return field[0].transpose(1, 2, 0, 3)
 
 
-def finish(gin_hbm, gq_hbm, gin_out, gq_out, sems):
-    copies = [
-        pltpu.make_async_copy(gin_hbm, gin_out, sems.at[0]),
-        pltpu.make_async_copy(gq_hbm, gq_out, sems.at[1]),
-    ]
-    for copy in copies:
-        copy.start()
-    for copy in copies:
-        copy.wait()
+def finish(gin_hbm, gq_hbm, gin_out, gq_out, gin_ref, gq_ref, in_sems, out_sems):
+    halves = []
+    for src, mid, dst in ((gin_hbm, gin_ref, gin_out), (gq_hbm, gq_ref, gq_out)):
+        size = src.shape[0] // 2
+        for k in range(2):
+            at = pl.ds(size * k, size)
+            n = len(halves)
+            halves.append((
+                pltpu.make_async_copy(src.at[at], mid.at[at], in_sems.at[n]),
+                pltpu.make_async_copy(mid.at[at], dst.at[at], out_sems.at[n])))
+    for load, _ in halves:
+        load.start()
+    for load, store in halves:
+        load.wait()
+        store.start()
+    for _, store in halves:
+        store.wait()
 
 
 def per_device(n_lat, n_lon, x_in, out_grad, w_qkv, w_proj, norm_gain, bias_table, lat_labels):
@@ -371,13 +355,12 @@
     cols, rows = outs // n_lat, features // n_lon
     chunk = 128 if cols % 128 == 0 else cols
     chunks, half = cols // chunk, n_lon // 2
-    order, ready = steps(features, cols, chunk, n_lat)
     vmem = pl.BlockSpec(memory_space=pltpu.VMEM)
     dma = lambda *shape: pltpu.SemaphoreType.DMA(shape)
     peers = max(n_lat - 1, 1)
     grid = (LAT, LON, LEV, features)
     grad_input, grad_qkv = pl.pallas_call(
-        functools.partial(kernel, n_lat, n_lon, chunk, order, ready),
+        functools.partial(kernel, n_lat, n_lon, chunk),
         out_shape=(
             jax.ShapeDtypeStruct(grid, BF),
             jax.ShapeDtypeStruct((rows, cols), F32),
@@ -430,7 +413,8 @@
         ),
         in_specs=[pl.BlockSpec(memory_space=pl.ANY)] * 2,
         out_specs=[pl.BlockSpec(memory_space=pl.ANY)] * 2,
-        scratch_shapes=[pltpu.SemaphoreType.DMA((2,))],
+        scratch_shapes=[
+            pltpu.VMEM(grid, BF), pltpu.VMEM((rows, cols), F32), dma(4), dma(4)],
     )(grad_input, grad_qkv)
     return grad_input.transpose(2, 0, 1, 3)[None], grad_qkv.T[None]
 

time: 52.7 us -> 42 us (0.80)
  Pallas kernels: 51.9 us -> 41.2 us
    pallas_call x1, Pallas kernels: 11.5 us -> 1.72 us  [per_device(): pl.pallas_call(finish, out_shape=(jax.ShapeDtypeStruct(grid, BF), jax.Sha...]
    pallas_call x1, Pallas kernels: 40.4 us -> 39.5 us  [per_device(): pl.pallas_call(functools.partial(kernel, n_lat, n_lon, chunk), out_shape=...]
where the time goes in v4:
time: 42 us; the launch traced here: 41.8 us
  Pallas kernels  41.2 us (98%)
  between operations  0.64 us (2%)
    pallas_call x1, Pallas kernels, per_device(): pl.pallas_call(functools.partial(kernel, n_lat, n_lon, chunk), out_shape=...  39.5 us
    pallas_call x1, Pallas kernels, per_device(): pl.pallas_call(finish, out_shape=(jax.ShapeDtypeStruct(grid, BF), jax.Sha...  1.72 us

profile of v4, /device:TPU:0, one launch (start us, length us, event | category | flops | bytes accessed | tf_op | source)
XLA Modules:
  0.0 41.8 jit_solution(12242567419691012974)
XLA Ops:
  0.6 39.5 %shard_map.95 = (bf16[6,12,2,512]{3,2,1,0:T(2,128)(2,1)}, f32[64,768]{1,0:T(8,128)}) custom-call(bf16[6,12,2,512]{3,2,1,0:T(2,128)(2,1)} %bitcast.17, bf16[6,12,2,512]{3,2,1,0:T(2,128)(2,1)} %bitcast.18, bf16[1536,512]{1,0:T(8,128)(2,1)} %bitcast.15, bf16[512,512]{1,0:T(8,128)(2,1)} %bitcast.16, f32[1,512]{1,0:T(1,128)} %gain_hbm.1, f32[8,759]{1,0:T(8,128)} %bitcast.19, ...), custom_call_target="tpu_custom_call" | custom-call | tf_op jit(solution)/shard_map/pallas_call | solution.py:362
  40.1 1.7 %shard_map.96 = (bf16[6,12,2,512]{3,2,1,0:T(2,128)(2,1)}, f32[64,768]{1,0:T(8,128)}) custom-call(bf16[6,12,2,512]{3,2,1,0:T(2,128)(2,1)} %get-tuple-element.6.gin_hbm, f32[64,768]{1,0:T(8,128)} %get-tuple-element.7.gq_hbm), custom_call_target="tpu_custom_call" | custom-call | tf_op jit(solution)/shard_map/pallas_call | solution.py:408

commit v5 on v4

--- a/solution.py
+++ b/solution.py
@@ -81,13 +81,23 @@
         (table_hbm, table_ref),
         (select_hbm, select_ref),
         (quadrant(x_hbm, 1, 1), quadrant(win_x, 0, 0)),
-        (quadrant(og_hbm, 1, 1), quadrant(win_og, 0, 0)),
         (gain_hbm, gain_ref),
         (wqkv_hbm, wqkv_ref),
+        (quadrant(og_hbm, 1, 1), quadrant(win_og, 0, 0)),
         (wproj_hbm, wproj_ref),
     )):
         loads.append(pltpu.make_async_copy(src, dst, local_s.at[k]))
         loads[-1].start()
+    pl.semaphore_wait(barrier, len(offsets) + 1)
+
+    halo = []
+    for src, dst in ((x_hbm, win_x), (og_hbm, win_og)):
+        for ih, jh in ((0, 0), (1, 0), (0, 1)):
+            k = len(halo)
+            halo.append(pltpu.make_async_remote_copy(
+                quadrant(src, ih, jh), quadrant(dst, 1 - ih, 1 - jh), halo_s.at[k], halo_r.at[k],
+                device_id=device(ih - 1, jh - 1), device_id_type=MESH))
+            halo[-1].start()
     loads[0].wait()
     lane = lax.broadcasted_iota(jnp.int32, (8, 128), 1)
     own_lab = jnp.zeros((8, 128), F32)
@@ -95,16 +105,6 @@
         own_lab = jnp.where(lane == i, labels_ref[i].astype(F32), own_lab)
     send_lab[...] = own_lab
 
-    pl.semaphore_wait(barrier, len(offsets) + 1)
-
-    halo = []
-    for ih, jh in ((0, 0), (0, 1), (1, 0)):
-        for src, dst in ((x_hbm, win_x), (og_hbm, win_og)):
-            k = len(halo)
-            halo.append(pltpu.make_async_remote_copy(
-                quadrant(src, ih, jh), quadrant(dst, 1 - ih, 1 - jh), halo_s.at[k], halo_r.at[k],
-                device_id=device(ih - 1, jh - 1), device_id_type=MESH))
-            halo[-1].start()
     lab_copy = pltpu.make_async_remote_copy(
         send_lab, recv_lab, lab_s.at[0], lab_r.at[0],
         device_id=device(-1, 0), device_id_type=MESH)
@@ -144,11 +144,10 @@
         one = jnp.concatenate([one, jnp.zeros((ROWS - CELLS, 128), F32)], axis=0)
         bias[h // 2, ROWS * (h % 2):ROWS * (h % 2 + 1), :] = jnp.where(allowed, one, MASKED)
 
-    for copy in loads[3:] + halo:
+    for copy in loads[3:6] + halo[:3]:
         copy.wait()
     to_win = select_ref[:WROWS, :LEV * CELLS].astype(BF)
     x = dot(to_win, win_x[...].reshape(LEV * CELLS, features))
-    og = dot(to_win, win_og[...].reshape(LEV * CELLS, features))
     gain = gain_ref[...]
     center = jnp.mean(x, axis=-1, keepdims=True)
     spread = jnp.mean(jnp.square(x - center), axis=-1, keepdims=True)
@@ -214,6 +213,9 @@
             - jnp.mean(d_normed, axis=-1, keepdims=True)
             - normed[own] * jnp.mean(d_normed * normed[own], axis=-1, keepdims=True))
 
+    for copy in loads[6:] + halo[3:]:
+        copy.wait()
+    og = dot(to_win, win_og[...].reshape(LEV * CELLS, features))
     totals, skips = [], []
     for p in range(LEV):
         og_p = og[ROWS * p:ROWS * (p + 1)]
@@ -270,17 +272,16 @@
     def _():
         skips[0].wait_recv()
         d_attended = attended_grad(0, skip[0])
-        all_lows = [attention_grad(0, d_attended, True)]
+        lows = attention_grad(0, d_attended, True)
+        cot[0] = (totals[0] + (skip[0].astype(F32) + input_grad(0, lows))).astype(BF)
         skips[1].wait_recv()
         d_attended = attended_grad(1, skip[1])
-        all_lows.append(attention_grad(1, d_attended, True))
+        lows = attention_grad(1, d_attended, True)
         for c in range(chunks):
             send_factors(c)
+        cot[1] = (totals[1] + (skip[1].astype(F32) + input_grad(1, lows))).astype(BF)
         for c in range(chunks):
             send_sums(c)
-        for p in range(LEV):
-            second = input_grad(p, all_lows[p])
-            cot[p] = (totals[p] + (skip[p].astype(F32) + second)).astype(BF)
 
     whole = cot[...].reshape(WROWS, features)
     back_src[...] = dot(to_win, whole, TN).astype(BF).reshape(LAT, LON, LEV, features)

time: 42 us -> 41.9 us (level)
  no operation moved by 1% of the time
where the time goes in v5:
time: 41.9 us; the launch traced here: 41.8 us
  Pallas kernels  41.1 us (98%)
  between operations  0.64 us (2%)
    pallas_call x1, Pallas kernels, per_device(): pl.pallas_call(functools.partial(kernel, n_lat, n_lon, chunk), out_shape=...  39.4 us
    pallas_call x1, Pallas kernels, per_device(): pl.pallas_call(finish, out_shape=(jax.ShapeDtypeStruct(grid, BF), jax.Sha...  1.72 us

profile of v5, /device:TPU:0, one launch (start us, length us, event | category | flops | bytes accessed | tf_op | source)
XLA Modules:
  0.0 41.8 jit_solution(154067549550194542)
XLA Ops:
  0.6 39.4 %shard_map.95 = (bf16[6,12,2,512]{3,2,1,0:T(2,128)(2,1)}, f32[64,768]{1,0:T(8,128)}) custom-call(bf16[6,12,2,512]{3,2,1,0:T(2,128)(2,1)} %bitcast.17, bf16[6,12,2,512]{3,2,1,0:T(2,128)(2,1)} %bitcast.18, bf16[1536,512]{1,0:T(8,128)(2,1)} %bitcast.15, bf16[512,512]{1,0:T(8,128)(2,1)} %bitcast.16, f32[1,512]{1,0:T(1,128)} %gain_hbm.1, f32[8,759]{1,0:T(8,128)} %bitcast.19, ...), custom_call_target="tpu_custom_call" | custom-call | tf_op jit(solution)/shard_map/pallas_call | solution.py:363
  40.1 1.7 %shard_map.96 = (bf16[6,12,2,512]{3,2,1,0:T(2,128)(2,1)}, f32[64,768]{1,0:T(8,128)}) custom-call(bf16[6,12,2,512]{3,2,1,0:T(2,128)(2,1)} %get-tuple-element.6.gin_hbm, f32[64,768]{1,0:T(8,128)} %get-tuple-element.7.gq_hbm), custom_call_target="tpu_custom_call" | custom-call | tf_op jit(solution)/shard_map/pallas_call | solution.py:409

commit v6 on v5

--- a/solution.py
+++ b/solution.py
@@ -43,16 +43,16 @@
 def kernel(
     n_lat, n_lon, chunk,
     x_hbm, og_hbm, wqkv_hbm, wproj_hbm, gain_hbm, table_hbm, labels_hbm, select_hbm,
-    gin_ref, gq_ref,
+    gin_ref, gq_hbm,
     win_x, win_og, wqkv_ref, wproj_ref, gain_ref, table_ref, labels_ref, select_ref,
-    send_lab, recv_lab, rolled, expanded, bias, proj, att, dqkv, cot, skip, back_src,
+    send_lab, recv_lab, rolled, expanded, bias, proj, att, dqkv, cot, skip, back_src, gq_ref,
     scaled, scaled_in, turned, low, low_in, part, part_in, summed, summed_in,
     local_s, halo_s, halo_r, lab_s, lab_r, skip_s, skip_r, back_s, back_r,
     sc_s, sc_r, low_s, low_r, pair_s, pair_r, grp_s, grp_r,
 ):
     ph, la, lo = lax.axis_index("phase"), lax.axis_index("lat"), lax.axis_index("lon")
     features = gain_ref.shape[-1]
-    rows, cols = gq_ref.shape
+    rows, cols = gq_hbm.shape
     half = n_lon // 2
     chunks = cols // chunk
     par = lax.rem(lo, 2)
@@ -291,7 +291,9 @@
         back.append(pltpu.make_async_remote_copy(
             quadrant(back_src, 1 - ih, 1 - jh), quadrant(gin_ref, ih, jh), back_s.at[k], back_r.at[k],
             device_id=device(1 - ih, 1 - jh), device_id_type=MESH))
-    gin_ref[LAT // 2:, LON // 2:] = back_src[:LAT // 2, :LON // 2]
+    results = [pltpu.make_async_copy(
+        quadrant(back_src, 0, 0), quadrant(gin_ref, 1, 1), local_s.at[0])]
+    results[0].start()
 
     for copy in back:
         copy.start()
@@ -312,13 +314,16 @@
         for d in range(1, half):
             groups[c * (half - 1) + d - 1].wait_recv()
             value = value + summed_in[c, d - 1].astype(F32)
-        gq_ref[:, chunk * c:chunk * (c + 1)] = value
+        at = pl.ds(chunk * c, chunk)
+        gq_ref[:, at] = value
+        results.append(pltpu.make_async_copy(gq_ref.at[:, at], gq_hbm.at[:, at], local_s.at[c + 1]))
+        results[-1].start()
 
     for copy in groups:
         copy.wait_send()
     for copy in pairs + [copy for step in low_copies for copy in step]:
         copy.wait_send()
-    for copy in back:
+    for copy in back + results:
         copy.wait()
 
     @pl.when(ph == 1)
@@ -356,7 +361,6 @@
     cols, rows = outs // n_lat, features // n_lon
     chunk = 128 if cols % 128 == 0 else cols
     chunks, half = cols // chunk, n_lon // 2
-    vmem = pl.BlockSpec(memory_space=pltpu.VMEM)
     dma = lambda *shape: pltpu.SemaphoreType.DMA(shape)
     peers = max(n_lat - 1, 1)
     grid = (LAT, LON, LEV, features)
@@ -367,7 +371,7 @@
             jax.ShapeDtypeStruct((rows, cols), F32),
         ),
         in_specs=[pl.BlockSpec(memory_space=pl.ANY)] * 8,
-        out_specs=(vmem, vmem),
+        out_specs=[pl.BlockSpec(memory_space=pl.ANY)] * 2,
         scratch_shapes=[
             pltpu.VMEM(grid, BF),
             pltpu.VMEM(grid, BF),
@@ -388,6 +392,7 @@
             pltpu.VMEM((LEV, ROWS, features), BF),
             pltpu.VMEM((LEV, ROWS, features), BF),
             pltpu.VMEM(grid, BF),
+            pltpu.VMEM((rows, cols), F32),
             pltpu.VMEM((WROWS, features), BF),
             pltpu.VMEM((peers, WROWS, features), BF),
             pltpu.VMEM((n_lat, features, WROWS), BF),
@@ -397,7 +402,7 @@
             pltpu.VMEM((chunks, half, rows, chunk), BF),
             pltpu.VMEM((chunks, half, rows, chunk), BF),
             pltpu.VMEM((chunks, half - 1, rows, chunk), BF),
-            dma(8), dma(6), dma(6), dma(1), dma(1), dma(LEV), dma(LEV), dma(3), dma(3),
+            dma(max(8, chunks + 1)), dma(6), dma(6), dma(1), dma(1), dma(LEV), dma(LEV), dma(3), dma(3),
             dma(peers), dma(peers), dma(peers, chunks), dma(peers, chunks),
             dma(chunks), dma(chunks), dma(chunks, half - 1), dma(chunks, half - 1),
         ],

time: 41.9 us -> 41.8 us (level)
  no operation moved by 1% of the time
where the time goes in v6:
time: 41.8 us; the launch traced here: 41.6 us
  Pallas kernels  41 us (98%)
  between operations  0.64 us (2%)
    pallas_call x1, Pallas kernels, per_device(): pl.pallas_call(functools.partial(kernel, n_lat, n_lon, chunk), out_shape=...  39.3 us
    pallas_call x1, Pallas kernels, per_device(): pl.pallas_call(finish, out_shape=(jax.ShapeDtypeStruct(grid, BF), jax.Sha...  1.72 us

profile of v6, /device:TPU:0, one launch (start us, length us, event | category | flops | bytes accessed | tf_op | source)
XLA Modules:
  0.0 41.6 jit_solution(12166321475796148139)
XLA Ops:
  0.6 39.3 %shard_map.95 = (bf16[6,12,2,512]{3,2,1,0:T(2,128)(2,1)}, f32[64,768]{1,0:T(8,128)}) custom-call(bf16[6,12,2,512]{3,2,1,0:T(2,128)(2,1)} %bitcast.17, bf16[6,12,2,512]{3,2,1,0:T(2,128)(2,1)} %bitcast.18, bf16[1536,512]{1,0:T(8,128)(2,1)} %bitcast.15, bf16[512,512]{1,0:T(8,128)(2,1)} %bitcast.16, f32[1,512]{1,0:T(1,128)} %gain_hbm.1, f32[8,759]{1,0:T(8,128)} %bitcast.19, ...), custom_call_target="tpu_custom_call" | custom-call | tf_op jit(solution)/shard_map/pallas_call | solution.py:367
  39.9 1.7 %shard_map.96 = (bf16[6,12,2,512]{3,2,1,0:T(2,128)(2,1)}, f32[64,768]{1,0:T(8,128)}) custom-call(bf16[6,12,2,512]{3,2,1,0:T(2,128)(2,1)} %get-tuple-element.6.gin_hbm, f32[64,768]{1,0:T(8,128)} %get-tuple-element.7.gq_hbm), custom_call_target="tpu_custom_call" | custom-call | tf_op jit(solution)/shard_map/pallas_call | solution.py:414
